TPU v7x, 32 devices: a whole 2x2x4 slice. The times are simulated.
32 devices in a mesh: batch: 8 (over z, x), seq: 4 (over y, core).
Axes of the slice: x: 2, y: 2, z: 4, core: 2. Of those that a mesh axis runs over, the one named last changes fastest.
Arguments:
- tokens_in: bfloat16 [16, 2048, 768], P('batch', 'seq'), may hold values from -6 to 6
- doc_starts: int32 [16, 6], P('batch'), may hold values from 0 to 2047, as said below
- mixer_in: bfloat16 [2, 768, 1920], P(None, 'batch'), may hold values from -0.21875 to 0.21875
- mixer_out: bfloat16 [2, 768, 768], P(None, 'batch'), may hold values from -0.21875 to 0.21875
- ffn_in: bfloat16 [2, 768, 3072], P(None, 'batch'), may hold values from -0.21875 to 0.21875
- ffn_out: bfloat16 [2, 1536, 768], P(None, 'batch'), may hold values from -0.15625 to 0.15625
- gains: float32 [2, 3, 768], replicated, may hold values from 0.5 to 1.5
- gate_params: float32 [2, 2, 384], replicated, as said below
- cotangent: bfloat16 [16, 2048, 768], P('batch', 'seq'), may hold values from -6 to 6
Outputs:
- block_out: bfloat16 [16, 2048, 768], P('batch', 'seq')
- d_tokens: float32 [16, 2048, 768], P('batch', 'seq')
- d_mixer_in: float32 [2, 768, 1920], P(None, 'batch')
- d_mixer_out: float32 [2, 768, 768], P(None, 'batch')
- d_ffn_in: float32 [2, 768, 3072], P(None, 'batch')
- d_ffn_out: float32 [2, 1536, 768], P(None, 'batch')
- d_gains: float32 [2, 3, 768], replicated
- d_gate_params: float32 [2, 2, 384], replicated
Inputs may be any that keep to these rules, and one draw needn't show every extreme that they name: `doc_starts`: along each row the starts do not fall and the first is 0; equal starts mark empty documents. gate_params[l, 0] are angles, gate_params[l, 1] lower bounds of the forget gates between 0 and 1.
All inputs are finite; a program needn't handle non-finite values.
Results may differ from a plain program's by a relative error of at most 0.02.
Values may be sent and summed in bfloat16 or wider, within the bound.
A program may use at most 256 MiB of HBM per device.

v0:
```python
import jax
import jax.numpy as jnp
from jax import lax
from jax.sharding import PartitionSpec as P

LAYERS = 2


EPS = 1e-06


def passed_along(block, axis, distance):
    devices = range(lax.axis_size(axis))
    route = [(i - distance, i) for i in devices if i - distance in devices]
    return lax.ppermute(block, axis, route)


def swish(values):
    return values * jax.nn.sigmoid(values)


def swish_slope(values):
    sigma = jax.nn.sigmoid(values)
    return sigma * (1.0 + values * (1.0 - sigma))


def rms_scale(values):
    return lax.rsqrt(jnp.mean(values * values, axis=-1, keepdims=True) + EPS)


def complex_combine(earlier, later_segment):
    earlier_acc_real, earlier_acc_imaginary, earlier_source_real, earlier_source_imaginary = earlier
    later_term_real, later_term_imaginary, later_source_real, later_source_imaginary = later_segment
    return (
        later_term_real * earlier_acc_real - later_term_imaginary * earlier_acc_imaginary,
        later_term_real * earlier_acc_imaginary + later_term_imaginary * earlier_acc_real,
        later_term_real * earlier_source_real
        - later_term_imaginary * earlier_source_imaginary
        + later_source_real,
        later_term_real * earlier_source_imaginary
        + later_term_imaginary * earlier_source_real
        + later_source_imaginary,
    )


def linear_chain(decay_r, decay_i, source_r, source_i):
    return lax.associative_scan(complex_combine, (decay_r, decay_i, source_r, source_i), axis=1)


def contract_rows(left, right):
    return lax.dot_general(
        left, right, (((0,), (0,)), ((), ())), preferred_element_type=jnp.float32
    )


def contract_cols(left, right):
    return lax.dot_general(
        left, right, (((1,), (1,)), ((), ())), preferred_element_type=jnp.float32
    )


def norm_back(d_out, normal, scale, gain):
    d_hat = d_out * gain
    d_gain = jnp.sum(d_out * normal, axis=0)
    d_in = scale * (d_hat - normal * jnp.mean(d_hat * normal, axis=-1, keepdims=True))
    return (d_in, d_gain)


def pass_states(element, forward):
    mult_r, mult_i, add_r, add_i = element

    def hop_step(count, incoming):
        out_r = mult_r * incoming[0] - mult_i * incoming[1] + add_r
        out_i = mult_r * incoming[1] + mult_i * incoming[0] + add_i
        outgoing = jnp.stack([out_r, out_i])
        if forward:
            return passed_along(outgoing, "seq", 1)
        return passed_along(outgoing, "seq", -1)

    start_value = jnp.zeros((2,) + mult_r.shape, jnp.float32)
    arrived = lax.fori_loop(0, lax.axis_size("seq") - 1, hop_step, start_value)
    return (arrived[0], arrived[1])


def layer_forward(stream, whole_weights, gain_rows, gate_pair, keep, rows):
    weight_in, weight_out, weight_ffn, weight_down = whole_weights
    chan = gate_pair.shape[1]
    token_count = stream.shape[0]
    length = token_count // rows
    scale_one = rms_scale(stream)
    normed = (stream * scale_one * gain_rows[0]).astype(jnp.bfloat16)
    projected = jnp.dot(normed, weight_in, preferred_element_type=jnp.float32)
    theta = gate_pair[0]
    lower = gate_pair[1]
    forget = jax.nn.sigmoid(projected[:, 2 * chan : 3 * chan])
    retain = keep * (lower + (1.0 - lower) * forget)
    decay_r = (retain * jnp.cos(theta)).reshape(rows, length, chan)
    decay_i = (retain * jnp.sin(theta)).reshape(rows, length, chan)
    source_r = ((1.0 - retain) * swish(projected[:, :chan])).reshape(rows, length, chan)
    source_i = ((1.0 - retain) * swish(projected[:, chan : 2 * chan])).reshape(rows, length, chan)
    cum_r, cum_i, local_r, local_i = linear_chain(decay_r, decay_i, source_r, source_i)
    carry_r, carry_i = pass_states(
        (cum_r[:, -1], cum_i[:, -1], local_r[:, -1], local_i[:, -1]), True
    )
    state_r = local_r + cum_r * carry_r[:, None] - cum_i * carry_i[:, None]
    state_i = local_i + cum_r * carry_i[:, None] + cum_i * carry_r[:, None]
    state = jnp.concatenate([state_r, state_i], axis=-1).reshape(token_count, 2 * chan)
    scale_two = rms_scale(state)
    gate_act = swish(projected[:, 3 * chan :])
    mixed = (state * scale_two * gain_rows[1] * gate_act).astype(jnp.bfloat16)
    middle = stream + jnp.dot(mixed, weight_out, preferred_element_type=jnp.float32)
    scale_three = rms_scale(middle)
    normed2 = (middle * scale_three * gain_rows[2]).astype(jnp.bfloat16)
    gate_up = jnp.dot(normed2, weight_ffn, preferred_element_type=jnp.float32)
    hidden_units = weight_down.shape[0]
    hidden = (swish(gate_up[:, :hidden_units]) * gate_up[:, hidden_units:]).astype(jnp.bfloat16)
    result = middle + jnp.dot(hidden, weight_down, preferred_element_type=jnp.float32)
    saved = (
        stream,
        scale_one,
        normed,
        projected,
        retain,
        forget,
        state_r,
        state_i,
        carry_r,
        carry_i,
        state,
        scale_two,
        mixed,
        middle,
        scale_three,
        normed2,
        gate_up,
        hidden,
    )
    return (result, saved)


def layer_backward(d_result, whole_weights, gain_rows, gate_pair, keep, rows, saved):
    weight_in, weight_out, weight_ffn, weight_down = whole_weights
    (
        stream,
        scale_one,
        normed,
        projected,
        retain,
        forget,
        state_r,
        state_i,
        carry_r,
        carry_i,
        state,
        scale_two,
        mixed,
        middle,
        scale_three,
        normed2,
        gate_up,
        hidden,
    ) = saved
    chan = gate_pair.shape[1]
    token_count = stream.shape[0]
    length = token_count // rows
    hidden_units = weight_down.shape[0]
    theta = gate_pair[0]
    lower = gate_pair[1]
    cos_theta = jnp.cos(theta)
    sin_theta = jnp.sin(theta)
    d_down = d_result.astype(jnp.bfloat16)
    d_weight_down = contract_rows(hidden, d_down)
    d_hidden = contract_cols(d_down, weight_down)
    gate_part = gate_up[:, :hidden_units]
    up_part = gate_up[:, hidden_units:]
    d_gate_up = jnp.concatenate(
        [d_hidden * up_part * swish_slope(gate_part), d_hidden * swish(gate_part)], axis=1
    ).astype(jnp.bfloat16)
    d_weight_ffn = contract_rows(normed2, d_gate_up)
    d_normed2 = contract_cols(d_gate_up, weight_ffn)
    from_norm, d_gain_two = norm_back(d_normed2, middle * scale_three, scale_three, gain_rows[2])
    d_middle = d_result + from_norm
    d_branch = d_middle.astype(jnp.bfloat16)
    d_weight_out = contract_rows(mixed, d_branch)
    d_mixed = contract_cols(d_branch, weight_out)
    part_g = projected[:, 3 * chan :]
    gate_act = swish(part_g)
    state_hat = state * scale_two
    d_part_g = d_mixed * state_hat * gain_rows[1] * swish_slope(part_g)
    d_state, d_gain_one = norm_back(d_mixed * gate_act, state_hat, scale_two, gain_rows[1])
    grad_r = d_state[:, :chan].reshape(rows, length, chan)
    grad_i = d_state[:, chan:].reshape(rows, length, chan)
    retain_rows = retain.reshape(rows, length, chan)
    step_r = retain_rows * cos_theta
    step_i = retain_rows * sin_theta
    next_r = jnp.concatenate([step_r[:, 1:], jnp.ones((rows, 1, chan), jnp.float32)], axis=1)
    next_i = jnp.concatenate([step_i[:, 1:], jnp.zeros((rows, 1, chan), jnp.float32)], axis=1)
    rev_q_r, rev_q_i, rev_g_r, rev_g_i = linear_chain(
        next_r[:, ::-1], -next_i[:, ::-1], grad_r[:, ::-1], grad_i[:, ::-1]
    )
    back_q_r = rev_q_r[:, ::-1]
    back_q_i = rev_q_i[:, ::-1]
    back_g_r = rev_g_r[:, ::-1]
    back_g_i = rev_g_i[:, ::-1]
    first_r = step_r[:, 0]
    first_i = -step_i[:, 0]
    element = (
        first_r * back_q_r[:, 0] - first_i * back_q_i[:, 0],
        first_r * back_q_i[:, 0] + first_i * back_q_r[:, 0],
        first_r * back_g_r[:, 0] - first_i * back_g_i[:, 0],
        first_r * back_g_i[:, 0] + first_i * back_g_r[:, 0],
    )
    income_r, income_i = pass_states(element, False)
    total_r = back_g_r + back_q_r * income_r[:, None] - back_q_i * income_i[:, None]
    total_i = back_g_i + back_q_r * income_i[:, None] + back_q_i * income_r[:, None]
    prior_r = jnp.concatenate([carry_r[:, None], state_r[:, :-1]], axis=1)
    prior_i = jnp.concatenate([carry_i[:, None], state_i[:, :-1]], axis=1)
    d_step_r = total_r * prior_r + total_i * prior_i
    d_step_i = total_i * prior_r - total_r * prior_i
    part_r = projected[:, :chan].reshape(rows, length, chan)
    part_i = projected[:, chan : 2 * chan].reshape(rows, length, chan)
    input_r = swish(part_r)
    input_i = swish(part_i)
    d_retain = d_step_r * cos_theta + d_step_i * sin_theta - (total_r * input_r + total_i * input_i)
    d_theta = jnp.sum(retain_rows * (d_step_i * cos_theta - d_step_r * sin_theta), axis=(0, 1))
    d_part_r = ((1.0 - retain_rows) * total_r * swish_slope(part_r)).reshape(token_count, chan)
    d_part_i = ((1.0 - retain_rows) * total_i * swish_slope(part_i)).reshape(token_count, chan)
    d_retain = d_retain.reshape(token_count, chan) * keep
    d_lower = jnp.sum(d_retain * (1.0 - forget), axis=0)
    d_part_f = d_retain * (1.0 - lower) * forget * (1.0 - forget)
    d_projected = jnp.concatenate([d_part_r, d_part_i, d_part_f, d_part_g], axis=1).astype(
        jnp.bfloat16
    )
    d_weight_in = contract_rows(normed, d_projected)
    d_normed = contract_cols(d_projected, weight_in)
    from_first, d_gain_zero = norm_back(d_normed, stream * scale_one, scale_one, gain_rows[0])
    d_stream = d_middle + from_first
    big_grads = (d_weight_in, d_weight_out, d_weight_ffn, d_weight_down)
    return (
        d_stream,
        big_grads,
        jnp.stack([d_gain_zero, d_gain_one, d_gain_two]),
        jnp.stack([d_theta, d_lower]),
    )


def shards(
    tokens_in, doc_starts, mixer_in, mixer_out, ffn_in, ffn_out, gains, gate_params, cotangent
):
    rows, length, width = tokens_in.shape
    positions = lax.axis_index("seq") * length + jnp.arange(length, dtype=jnp.int32)
    resets = jnp.any(doc_starts[:, :, None] == positions[None, None, :], axis=1)
    keep = (1.0 - resets.astype(jnp.float32)).reshape(rows * length, 1)
    stream = tokens_in.astype(jnp.float32).reshape(rows * length, width)
    saved_layers = []
    for which_layer in range(LAYERS):
        whole_weights = (
            lax.all_gather(mixer_in[which_layer], "batch", axis=0, tiled=True),
            lax.all_gather(mixer_out[which_layer], "batch", axis=0, tiled=True),
            lax.all_gather(ffn_in[which_layer], "batch", axis=0, tiled=True),
            lax.all_gather(ffn_out[which_layer], "batch", axis=0, tiled=True),
        )
        stream, saved = layer_forward(
            stream, whole_weights, gains[which_layer], gate_params[which_layer], keep, rows
        )
        saved_layers.append(saved)
    block_out = stream.reshape(rows, length, width).astype(jnp.bfloat16)
    d_stream = cotangent.astype(jnp.float32).reshape(rows * length, width)
    big_list = [None] * LAYERS
    gain_list = [None] * LAYERS
    pair_list = [None] * LAYERS
    for which_layer in reversed(range(LAYERS)):
        whole_weights = (
            lax.all_gather(mixer_in[which_layer], "batch", axis=0, tiled=True),
            lax.all_gather(mixer_out[which_layer], "batch", axis=0, tiled=True),
            lax.all_gather(ffn_in[which_layer], "batch", axis=0, tiled=True),
            lax.all_gather(ffn_out[which_layer], "batch", axis=0, tiled=True),
        )
        d_stream, big_grads, gain_grad, pair_grad = layer_backward(
            d_stream,
            whole_weights,
            gains[which_layer],
            gate_params[which_layer],
            keep,
            rows,
            saved_layers[which_layer],
        )
        shares = (
            lax.psum_scatter(
                big_grads[0].astype(jnp.bfloat16), "batch", scatter_dimension=0, tiled=True
            ).astype(jnp.float32),
            lax.psum_scatter(
                big_grads[1].astype(jnp.bfloat16), "batch", scatter_dimension=0, tiled=True
            ).astype(jnp.float32),
            lax.psum_scatter(
                big_grads[2].astype(jnp.bfloat16), "batch", scatter_dimension=0, tiled=True
            ).astype(jnp.float32),
            lax.psum_scatter(
                big_grads[3].astype(jnp.bfloat16), "batch", scatter_dimension=0, tiled=True
            ).astype(jnp.float32),
        )
        big_list[which_layer] = (
            lax.psum(shares[0].astype(jnp.bfloat16), "seq").astype(jnp.float32),
            lax.psum(shares[1].astype(jnp.bfloat16), "seq").astype(jnp.float32),
            lax.psum(shares[2].astype(jnp.bfloat16), "seq").astype(jnp.float32),
            lax.psum(shares[3].astype(jnp.bfloat16), "seq").astype(jnp.float32),
        )
        gain_list[which_layer] = gain_grad
        pair_list[which_layer] = pair_grad
    gain_local = jnp.stack(gain_list)
    pair_local = jnp.stack(pair_list)
    d_gains, d_gate_params = lax.psum((gain_local, pair_local), ("batch", "seq"))
    d_tokens = d_stream.reshape(rows, length, width)
    d_mixer_in = jnp.stack([big_list[k][0] for k in range(LAYERS)])
    d_mixer_out = jnp.stack([big_list[k][1] for k in range(LAYERS)])
    d_ffn_in = jnp.stack([big_list[k][2] for k in range(LAYERS)])
    d_ffn_out = jnp.stack([big_list[k][3] for k in range(LAYERS)])
    return (
        block_out,
        d_tokens,
        d_mixer_in,
        d_mixer_out,
        d_ffn_in,
        d_ffn_out,
        d_gains,
        d_gate_params,
    )


def solution(mesh):
    in_specs = (
        P("batch", "seq", None),
        P("batch", None),
        P(None, "batch", None),
        P(None, "batch", None),
        P(None, "batch", None),
        P(None, "batch", None),
        P(),
        P(),
        P("batch", "seq", None),
    )
    out_specs = (
        P("batch", "seq", None),
        P("batch", "seq", None),
        P(None, "batch", None),
        P(None, "batch", None),
        P(None, "batch", None),
        P(None, "batch", None),
        P(),
        P(),
    )
    return jax.shard_map(shards, mesh=mesh, in_specs=in_specs, out_specs=out_specs, check_vma=False)
```

profile of v0, /device:TPU:0, one launch (start us, length us, event | category | flops | bytes accessed | tf_op | source)
XLA Modules:
  0.0 2126.0 jit_solution(5767610060869116278)
XLA Ops:
  18.1 53.7 %all-gather.17.cloned.1.call-done = bf16[1,768,1920]{2,1,0:T(8,128)(2,1)} async-done(((bf16[1,96,1920]{2,1,0:T(8,128)(2,1)}), bf16[1,768,1920]{2,1,0:T(8,128)(2,1)}) %all-gather.17.cloned.1.call-update) | async-done | bytes 2949136 | tf_op jit(solution)/shard_map/all_gather | solution.py:258
  422.0 12.1 while.40
  451.9 8.0 fusion.16
  722.3 7.7 rev.36
  796.4 14.7 while.41
  828.0 11.2 fusion.12
  839.2 10.4 multiply_convert_fusion.3
  1193.0 15.3 while.42
  1208.3 7.8 rev.37
  1216.1 7.8 rev.38
  1224.0 13.0 rev.40
  1258.4 8.6 multiply_convert_fusion.1
  1267.0 11.2 multiply_reduce_fusion.3
  1621.9 12.8 rev.44
  1711.3 12.8 rev.42
  1724.2 7.8 rev.43
  1732.0 12.9 rev.45
  1744.9 14.9 while.43
  1777.6 10.3 convolution_convert_fusion
  1789.9 10.2 convolution_convert_fusion.1
  1809.6 41.8 %all-reduce.294 = (f32[2,3,768]{2,1,0:T(4,128)S(1)}, f32[2,2,384]{2,1,0:T(2,128)}) all-reduce(f32[2,3,768]{2,1,0:T(4,128)S(1)} %pad_maximum_fusion.116, f32[2,2,384]{2,1,0:T(2,128)S(1)} %pad_maximum_fusion.149), channel_id=1, replica_groups=mesh['batch'=8,'seq'=4] {'batch','seq'}, use_global_device_ids=true, to_apply=%region_43.0 | all-reduce | flops 6144 | bytes 49152 | tf_op jit(solution)/shard_map/psum | solution.py:312
  1852.0 95.4 %reduce-scatter.19.cloned.1.call-done = bf16[96,3072]{1,0:T(8,128)(2,1)} async-done(((bf16[768,3072]{1,0:T(8,128)(2,1)}), bf16[96,3072]{1,0:T(8,128)(2,1)}) %reduce-scatter.19.cloned.1.call-update) | async-done | bytes 589840 | tf_op jit(solution)/shard_map/reduce_scatter | solution.py:295
  1947.5 98.7 %reduce-scatter.17.cloned.1.call-done = bf16[96,3072]{1,0:T(8,128)(2,1)} async-done(((bf16[768,3072]{1,0:T(8,128)(2,1)}), bf16[96,3072]{1,0:T(8,128)(2,1)}) %reduce-scatter.17.cloned.1.call-update) | async-done | bytes 589840 | tf_op jit(solution)/shard_map/reduce_scatter | solution.py:295
  2056.4 56.6 %all-reduce.298.cloned.1.call-done = (bf16[1,96,1920]{2,1,0:T(8,128)(2,1)}, bf16[1,96,1920]{2,1,0:T(8,128)(2,1)}, bf16[1,96,768]{2,1,0:T(8,128)(2,1)}, bf16[1,96...) async-done(((bf16[1,96,1920]{2,1,0:T(8,128)(2,1)}, ...) | async-done | bytes 2801680 | tf_op jit(solution)/shard_map/psum | solution.py:303
  (2323 shorter events, 1604.7 us)
Async XLA Ops:
  7.2 64.7 %all-gather.17.cloned.1.call-start = ((), (), s32[]{:S(2)}) async-start(), calls=%async_computation.16 | async-start | bytes 3317760 | tf_op jit(solution)/shard_map/all_gather | solution.py:258
  9.4 437.0 %all-gather.19.cloned.1.call-start = ((), (), s32[]{:S(2)}) async-start(), calls=%async_computation.17 | async-start | bytes 1327104 | tf_op jit(solution)/shard_map/all_gather | solution.py:259
  10.2 441.1 %all-gather.21.cloned.1.call-start = ((), (), s32[]{:S(2)}) async-start(), calls=%async_computation.18 | async-start | bytes 5308416 | tf_op jit(solution)/shard_map/all_gather | solution.py:260
  11.4 456.5 %all-gather.23.cloned.1.call-start = ((), (), s32[]{:S(2)}) async-start(), calls=%async_computation.19 | async-start | bytes 2654208 | tf_op jit(solution)/shard_map/all_gather | solution.py:261
  12.4 462.5 %all-gather.25.cloned.1.call-start = ((), (), s32[]{:S(2)}) async-start(), calls=%async_computation.20 | async-start | bytes 3317760 | tf_op jit(solution)/shard_map/all_gather | solution.py:258
  13.0 809.2 %all-gather.27.cloned.1.call-start = ((), (), s32[]{:S(2)}) async-start(), calls=%async_computation.21 | async-start | bytes 1327104 | tf_op jit(solution)/shard_map/all_gather | solution.py:259
  13.6 814.5 %all-gather.29.cloned.1.call-start = ((), (), s32[]{:S(2)}) async-start(), calls=%async_computation.22 | async-start | bytes 5308416 | tf_op jit(solution)/shard_map/all_gather | solution.py:260
  14.3 824.9 %all-gather.31.cloned.1.call-start = ((), (), s32[]{:S(2)}) async-start(), calls=%async_computation.23 | async-start | bytes 2654208 | tf_op jit(solution)/shard_map/all_gather | solution.py:261
  15.1 1836.9 %reduce-scatter.15.cloned.1.call-start = ((), (), s32[]{:S(2)}) async-start(), calls=%async_computation.11 | async-start | bytes 1327104 | tf_op jit(solution)/shard_map/reduce_scatter | solution.py:292
  424.1 4.9 collective-permute-start
  429.1 4.9 collective-permute-start
  806.2 4.9 collective-permute-start.1
  1197.8 5.5 collective-permute-start.2
  1203.4 4.9 collective-permute-start.2
  1278.2 573.8 %reduce-scatter.13.cloned.1.call-start = ((), (), s32[]{:S(2)}) async-start(), calls=%async_computation.10 | async-start | bytes 1327104 | tf_op jit(solution)/shard_map/reduce_scatter | solution.py:292
  1378.6 473.4 %reduce-scatter.23.cloned.1.call-start = ((), (), s32[]{:S(2)}) async-start(), calls=%async_computation.15 | async-start | bytes 2654208 | tf_op jit(solution)/shard_map/reduce_scatter | solution.py:298
  1473.3 378.7 %reduce-scatter.21.cloned.1.call-start = ((), (), s32[]{:S(2)}) async-start(), calls=%async_computation.14 | async-start | bytes 2654208 | tf_op jit(solution)/shard_map/reduce_scatter | solution.py:298
  1598.5 253.5 %reduce-scatter.11.cloned.1.call-start = ((), (), s32[]{:S(2)}) async-start(), calls=%async_computation.9 | async-start | bytes 3317760 | tf_op jit(solution)/shard_map/reduce_scatter | solution.py:289
  1677.4 174.7 %reduce-scatter.9.cloned.1.call-start = ((), (), s32[]{:S(2)}) async-start(), calls=%async_computation.8 | async-start | bytes 3317760 | tf_op jit(solution)/shard_map/reduce_scatter | solution.py:289
  1744.9 5.0 collective-permute-start.3
  1749.9 4.9 collective-permute-start.3
  1777.0 170.5 %reduce-scatter.19.cloned.1.call-start = ((), (), s32[]{:S(2)}) async-start(), calls=%async_computation.13 | async-start | bytes 5308416 | tf_op jit(solution)/shard_map/reduce_scatter | solution.py:295
  1788.0 258.2 %reduce-scatter.17.cloned.1.call-start = ((), (), s32[]{:S(2)}) async-start(), calls=%async_computation.12 | async-start | bytes 5308416 | tf_op jit(solution)/shard_map/reduce_scatter | solution.py:295
  1800.2 312.8 %all-reduce.298.cloned.1.call-start = ((), (), s32[]{:S(2)}) async-start(), calls=%async_computation.24 | async-start | bytes 5603328 | tf_op jit(solution)/shard_map/psum | solution.py:303
  (481 other events, 4139.0 us)
Sparse Core Ops, SparseCore 0:
  10.8 61.0 all-gather.16
  74.1 39.6 all-gather.18
  116.0 78.6 all-gather.20
  196.7 50.2 all-gather.22
  249.0 56.8 all-gather.24
  308.0 39.6 all-gather.26
  350.4 78.6 all-gather.28
  431.3 50.2 all-gather.30
  1278.3 63.7 reduce-scatter.14
  1378.7 63.7 reduce-scatter.12
  1473.4 68.7 reduce-scatter.22
  1598.6 68.9 reduce-scatter.20
  1677.5 72.1 reduce-scatter.10
  1777.1 72.3 reduce-scatter.8
  1853.0 94.4 reduce-scatter.18
  1951.0 95.1 reduce-scatter.16
  2049.0 64.0 all-reduce.297
where the time goes:
time: 2170 us; the launch traced here: 2130 us
  local copies, waits for them, and re-layouts  1210 us (56%)
  waiting for transfers between devices  334 us (15%)
  other arithmetic  324 us (15%)
  matrix products  166 us (8%)
  blocking collectives  41.8 us (2%)
  starting transfers between devices  30.4 us (1%)
  between operations  22.4 us (1%)
    slice x508, local copies, waits for them, and re-layouts, linear_chain(): lax.associative_scan(complex_combine, (decay_r, decay_i, source_r, source...  910 us
    reduce_scatter x2, waiting for transfers between devices, shards(): lax.psum_scatter(big_grads[2].astype(jnp.bfloat16), 'batch', scatter_dime...  194 us
    pad x256, local copies, waits for them, and re-layouts, linear_chain(): lax.associative_scan(complex_combine, (decay_r, decay_i, source_r, source...  139 us
    add x54, other arithmetic, complex_combine(): later_term_real * earlier_source_imaginary  75.7 us
    add x144, other arithmetic, linear_chain(): lax.associative_scan(complex_combine, (decay_r, decay_i, source_r, source...  70.8 us
    dot_general x8, matrix products, contract_cols(): lax.dot_general(left, right, (((1,), (1,)), ((), ())), preferred_element_...  61.4 us
    psum x1, waiting for transfers between devices, shards(): lax.psum(shares[0].astype(jnp.bfloat16), 'seq').astype(jnp.float32)  56.6 us
    all_gather x2, waiting for transfers between devices, shards(): lax.all_gather(mixer_in[which_layer], 'batch', axis=0, tiled=True)  53.8 us
  transfers between devices with their start and end apart: 29, of which 16 were waited for; matrix products, arithmetic and copies ran while one was open for 58% of the time, Pallas kernels for 0%

commit v1 on v0

v1 whole, which is shorter than its diff:
```python
import functools

import jax
import jax.numpy as jnp
from jax import lax
from jax.experimental import pallas as pl
from jax.experimental.pallas import tpu as pltpu
from jax.sharding import PartitionSpec as P

LAYERS = 2
EPS = 1e-06
F32 = jnp.float32
BF16 = jnp.bfloat16
LANES = 128
MESH = pl.DeviceIdType.MESH


def sigmoid(values):
    return 1.0 / (1.0 + jnp.exp(-values))


def rms_scale(values):
    return lax.rsqrt(jnp.mean(values * values, axis=-1, keepdims=True) + EPS)


def dot(left, right):
    return jnp.dot(left, right, preferred_element_type=F32)


def dot_t(left, right):
    return lax.dot_general(left, right, (((1,), (1,)), ((), ())), preferred_element_type=F32)


def eight_sum(values):
    rows, cols = values.shape
    return jnp.sum(values.reshape(rows // 8, 8, cols), axis=0)


def wide(ref, first, last):
    return jnp.concatenate([ref[g] for g in range(first, last)], axis=-1)


def split_store(ref, first, values):
    for g in range(values.shape[1] // LANES):
        ref[first + g] = values[:, g * LANES : (g + 1) * LANES]


def lanes(values):
    return [values[:, g * LANES : (g + 1) * LANES] for g in range(values.shape[1] // LANES)]


def keep_mask(rel_ref, row, first, shape):
    pos = lax.broadcasted_iota(jnp.int32, shape, 0) + first
    hit = pos == rel_ref[row, 0]
    for k in range(1, rel_ref.shape[1]):
        hit = hit | (pos == rel_ref[row, k])
    return hit


def enter_kernel(rel_ref, x_ref, w_ref, gain_ref, gate_ref, proj_ref, normed_ref, lam_ref, h_ref,
                 cum_ref, ends_ref, tot_ref, src):
    row, tile = pl.program_id(0), pl.program_id(1)
    tokens, width = x_ref.shape
    chan = width // 2
    seg = tokens // 8
    x = x_ref[...].astype(F32)
    normed = (x * rms_scale(x) * gain_ref[0:1, :]).astype(BF16)
    normed_ref[...] = normed
    proj = dot(normed, w_ref[...])
    proj_ref[...] = proj.astype(BF16)
    cos, sin, lower = gate_ref[0:1, :], gate_ref[1:2, :], gate_ref[2:3, :]
    seg_cos, seg_sin = gate_ref[3:4, :], gate_ref[4:5, :]
    p_r, p_i, p_f = proj[:, :chan], proj[:, chan : 2 * chan], proj[:, 2 * chan : 3 * chan]
    hit = keep_mask(rel_ref, row, tile * tokens, (tokens, chan))
    lam = jnp.where(hit, 0.0, lower + (1.0 - lower) * sigmoid(p_f))
    groups = chan // LANES
    split_store(lam_ref, 0, lam)
    split_store(src, 0, (1.0 - lam) * (p_r * sigmoid(p_r)))
    split_store(src, groups, (1.0 - lam) * (p_i * sigmoid(p_i)))
    cos_l, sin_l = lanes(cos), lanes(sin)

    def step(s, state):
        at = pl.ds(s, 8, stride=seg)
        after = []
        for k, (h_r, h_i, cum) in enumerate(state):
            lam_s = lam_ref[k, at, :]
            a_r, a_i = lam_s * cos_l[k], lam_s * sin_l[k]
            n_r = a_r * h_r - a_i * h_i + src[k, at, :]
            n_i = a_r * h_i + a_i * h_r + src[groups + k, at, :]
            cum = cum * lam_s
            h_ref[k, at, :] = n_r
            h_ref[groups + k, at, :] = n_i
            cum_ref[k, at, :] = cum
            after.append((n_r, n_i, cum))
        return tuple(after)

    zero = lam_ref[0, 0:8, :] * 0.0
    last = lax.fori_loop(0, seg, step, ((zero, zero, zero + 1.0),) * groups, unroll=8)
    e_r, e_i, e_c = (jnp.concatenate([v[i] for v in last], axis=-1) for i in range(3))
    ends_ref[0, 0:8, :] = e_r
    ends_ref[0, 8:16, :] = e_i
    ends_ref[0, 16:24, :] = e_c

    @pl.when(tile == 0)
    def _():
        tot_ref[0, 0:2, :] = jnp.zeros((2, chan), F32)
        tot_ref[0, 2:3, :] = jnp.ones((1, chan), F32)

    c_r, c_i, c_l = tot_ref[0, 0:1, :], tot_ref[0, 1:2, :], tot_ref[0, 2:3, :]
    for j in range(8):
        m = e_c[j : j + 1, :]
        a_r, a_i = m * seg_cos, m * seg_sin
        c_r, c_i = a_r * c_r - a_i * c_i + e_r[j : j + 1, :], a_r * c_i + a_i * c_r + e_i[j : j + 1, :]
        c_l = c_l * m
    tot_ref[0, 0:1, :] = c_r
    tot_ref[0, 1:2, :] = c_i
    tot_ref[0, 2:3, :] = c_l


def leave_kernel(x_ref, proj_ref, h_ref, cum_ref, ends_ref, carry_ref, wo_ref, wf_ref, wd_ref,
                 gain_ref, gate_ref, state_ref, prior_ref, mixed_ref, mid_ref, normed_ref, gu_ref,
                 hid_ref, out_ref, run):
    tile = pl.program_id(1)
    tokens, width = x_ref.shape
    chan = width // 2
    seg = tokens // 8
    cos, sin = gate_ref[0:1, :], gate_ref[1:2, :]
    seg_cos, seg_sin = gate_ref[3:4, :], gate_ref[4:5, :]

    @pl.when(tile == 0)
    def _():
        run[0:2, :] = carry_ref[0, 0:2, :]

    c_r, c_i = run[0:1, :], run[1:2, :]
    l_r, l_i = [], []
    for j in range(8):
        l_r.append(c_r)
        l_i.append(c_i)
        m = ends_ref[0, 16 + j : 17 + j, :]
        a_r, a_i = m * seg_cos, m * seg_sin
        c_r, c_i = (
            a_r * c_r - a_i * c_i + ends_ref[0, j : j + 1, :],
            a_r * c_i + a_i * c_r + ends_ref[0, 8 + j : 9 + j, :],
        )
    run[0:1, :] = c_r
    run[1:2, :] = c_i
    groups = chan // LANES
    start_r, start_i = lanes(jnp.concatenate(l_r, axis=0)), lanes(jnp.concatenate(l_i, axis=0))
    cos_l, sin_l = lanes(cos), lanes(sin)

    def step(s, state):
        at = pl.ds(s, 8, stride=seg)
        after = []
        for k, (w_r, w_i, q_r, q_i) in enumerate(state):
            w_r, w_i = w_r * cos_l[k] - w_i * sin_l[k], w_r * sin_l[k] + w_i * cos_l[k]
            cum = cum_ref[k, at, :]
            s_r = h_ref[k, at, :] + cum * w_r
            s_i = h_ref[groups + k, at, :] + cum * w_i
            state_ref[k, at, :] = s_r
            state_ref[groups + k, at, :] = s_i
            prior_ref[k, at, :] = q_r
            prior_ref[groups + k, at, :] = q_i
            after.append((w_r, w_i, s_r, s_i))
        return tuple(after)

    lax.fori_loop(0, seg, step, tuple(zip(start_r, start_i, start_r, start_i)), unroll=8)
    state = wide(state_ref, 0, 2 * groups)
    p_g = proj_ref[...].astype(F32)
    mixed = (state * rms_scale(state) * gain_ref[1:2, :] * (p_g * sigmoid(p_g))).astype(BF16)
    mixed_ref[...] = mixed
    mid = x_ref[...].astype(F32) + dot(mixed, wo_ref[...])
    mid_ref[...] = mid
    normed = (mid * rms_scale(mid) * gain_ref[2:3, :]).astype(BF16)
    normed_ref[...] = normed
    gu = dot(normed, wf_ref[...])
    gu_ref[...] = gu.astype(BF16)
    hidden = gu.shape[1] // 2
    gate = gu[:, :hidden]
    hid = (gate * sigmoid(gate) * gu[:, hidden:]).astype(BF16)
    hid_ref[...] = hid
    out_ref[...] = (mid + dot(hid, wd_ref[...])).astype(out_ref.dtype)


def back_out_kernel(dx_ref, gu_ref, mid_ref, state_ref, proj_ref, lam_ref, wo_ref, wf_ref, wd_ref,
                    gain_ref, gate_ref, dz_ref, dgu_ref, dmid_ref, dy_ref, dpg_ref, g_ref, cum_ref,
                    ends_ref, tot_ref, dgain_ref, grad):
    row, tile = pl.program_id(0), pl.program_id(1)
    tokens, width = dx_ref.shape
    chan = width // 2
    seg = tokens // 8
    cos, sin = gate_ref[0:1, :], gate_ref[1:2, :]
    seg_cos, seg_sin = gate_ref[3:4, :], gate_ref[4:5, :]
    dx = dx_ref[...].astype(F32)
    dz = dx.astype(BF16)
    dz_ref[...] = dz
    d_hid = dot_t(dz, wd_ref[...])
    hidden = d_hid.shape[1]
    gate = gu_ref[:, :hidden].astype(F32)
    up = gu_ref[:, hidden:].astype(F32)
    sg = sigmoid(gate)
    silu = gate * sg
    d_gu = jnp.concatenate(
        [(d_hid * up * (sg + silu * (1.0 - sg))).astype(BF16), (d_hid * silu).astype(BF16)], axis=1
    )
    dgu_ref[...] = d_gu
    d_n = dot_t(d_gu, wf_ref[...])
    mid = mid_ref[...]
    scale = rms_scale(mid)
    hat = mid * scale
    d_hat = d_n * gain_ref[2:3, :]

    @pl.when((row == 0) & (tile == 0))
    def _():
        dgain_ref[...] = jnp.zeros_like(dgain_ref)

    dgain_ref[8:16, :] += eight_sum(d_n * hat)
    d_mid = dx + scale * (d_hat - hat * jnp.mean(d_hat * hat, axis=-1, keepdims=True))
    dmid_ref[...] = d_mid
    dy = d_mid.astype(BF16)
    dy_ref[...] = dy
    d_mixed = dot_t(dy, wo_ref[...])
    p_g = proj_ref[...].astype(F32)
    sg = sigmoid(p_g)
    silu = p_g * sg
    groups = chan // LANES
    state = wide(state_ref, 0, 2 * groups)
    scale = rms_scale(state)
    hat = state * scale
    g1 = gain_ref[1:2, :]
    dpg_ref[...] = (d_mixed * hat * g1 * (sg + silu * (1.0 - sg))).astype(BF16)
    d_n = d_mixed * silu
    dgain_ref[0:8, :] += eight_sum(d_n * hat)
    d_hat = d_n * g1
    split_store(grad, 0, scale * (d_hat - hat * jnp.mean(d_hat * hat, axis=-1, keepdims=True)))
    cos_l, sin_l = lanes(cos), lanes(sin)

    def step(s, state):
        at = pl.ds(seg - 1 - s, 8, stride=seg)
        after = []
        for k, (g_r, g_i, cum, lam_n) in enumerate(state):
            a_r, a_i = lam_n * cos_l[k], lam_n * sin_l[k]
            n_r = grad[k, at, :] + a_r * g_r + a_i * g_i
            n_i = grad[groups + k, at, :] + a_r * g_i - a_i * g_r
            cum = cum * lam_n
            g_ref[k, at, :] = n_r
            g_ref[groups + k, at, :] = n_i
            cum_ref[k, at, :] = cum
            after.append((n_r, n_i, cum, lam_ref[k, at, :]))
        return tuple(after)

    zero = lam_ref[0, 0:8, :] * 0.0
    last = lax.fori_loop(0, seg, step, ((zero, zero, zero + 1.0, zero + 1.0),) * groups, unroll=8)
    g_r, g_i, cum, lam_0 = (jnp.concatenate([v[i] for v in last], axis=-1) for i in range(4))
    e_r = lam_0 * (cos * g_r + sin * g_i)
    e_i = lam_0 * (cos * g_i - sin * g_r)
    e_c = lam_0 * cum
    ends_ref[0, 0:8, :] = e_r
    ends_ref[0, 8:16, :] = e_i
    ends_ref[0, 16:24, :] = e_c

    @pl.when(tile == 0)
    def _():
        tot_ref[0, 0:2, :] = jnp.zeros((2, chan), F32)
        tot_ref[0, 2:3, :] = jnp.ones((1, chan), F32)

    c_r, c_i, c_l = tot_ref[0, 0:1, :], tot_ref[0, 1:2, :], tot_ref[0, 2:3, :]
    for j in reversed(range(8)):
        m = e_c[j : j + 1, :]
        a_r, a_i = m * seg_cos, m * seg_sin
        c_r, c_i = a_r * c_r + a_i * c_i + e_r[j : j + 1, :], a_r * c_i - a_i * c_r + e_i[j : j + 1, :]
        c_l = c_l * m
    tot_ref[0, 0:1, :] = c_r
    tot_ref[0, 1:2, :] = c_i
    tot_ref[0, 2:3, :] = c_l


def back_in_kernel(rel_ref, x_ref, dmid_ref, proj_ref, dpg_ref, lam_ref, prior_ref, g_ref, cum_ref,
                   ends_ref, carry_ref, w_ref, gain_ref, gate_ref, dproj_ref, dx_ref, dgain_ref,
                   dgate_ref, run, tot):
    row, tile = pl.program_id(0), pl.program_id(1)
    tokens, width = x_ref.shape
    chan = width // 2
    seg = tokens // 8
    cos, sin, lower = gate_ref[0:1, :], gate_ref[1:2, :], gate_ref[2:3, :]
    seg_cos, seg_sin = gate_ref[3:4, :], gate_ref[4:5, :]

    @pl.when(tile == 0)
    def _():
        run[0:2, :] = carry_ref[0, 0:2, :]

    c_r, c_i = run[0:1, :], run[1:2, :]
    l_r, l_i = [None] * 8, [None] * 8
    for j in reversed(range(8)):
        l_r[j], l_i[j] = c_r, c_i
        m = ends_ref[0, 16 + j : 17 + j, :]
        a_r, a_i = m * seg_cos, m * seg_sin
        c_r, c_i = (
            a_r * c_r + a_i * c_i + ends_ref[0, j : j + 1, :],
            a_r * c_i - a_i * c_r + ends_ref[0, 8 + j : 9 + j, :],
        )
    run[0:1, :] = c_r
    run[1:2, :] = c_i

    groups = chan // LANES
    start_r, start_i = lanes(jnp.concatenate(l_r, axis=0)), lanes(jnp.concatenate(l_i, axis=0))
    cos_l, sin_l = lanes(cos), lanes(sin)

    def step(s, state):
        at = pl.ds(seg - 1 - s, 8, stride=seg)
        after = []
        for k, (w_r, w_i) in enumerate(state):
            cum = cum_ref[k, at, :]
            tot[k, at, :] = g_ref[k, at, :] + cum * w_r
            tot[groups + k, at, :] = g_ref[groups + k, at, :] + cum * w_i
            after.append((w_r * cos_l[k] + w_i * sin_l[k], w_i * cos_l[k] - w_r * sin_l[k]))
        return tuple(after)

    lax.fori_loop(0, seg, step, tuple(zip(start_r, start_i)), unroll=8)
    g_r, g_i = wide(tot, 0, groups), wide(tot, groups, 2 * groups)
    q_r, q_i = wide(prior_ref, 0, groups), wide(prior_ref, groups, 2 * groups)
    p_r = proj_ref[:, :chan].astype(F32)
    p_i = proj_ref[:, chan : 2 * chan].astype(F32)
    forget = sigmoid(proj_ref[:, 2 * chan : 3 * chan].astype(F32))
    lam = wide(lam_ref, 0, groups)
    d_ar = g_r * q_r + g_i * q_i
    d_ai = g_i * q_r - g_r * q_i
    s_r, s_i = sigmoid(p_r), sigmoid(p_i)
    in_r, in_i = p_r * s_r, p_i * s_i
    d_lam = d_ar * cos + d_ai * sin - (g_r * in_r + g_i * in_i)

    @pl.when((row == 0) & (tile == 0))
    def _():
        dgain_ref[...] = jnp.zeros_like(dgain_ref)
        dgate_ref[...] = jnp.zeros_like(dgate_ref)

    dgate_ref[0:8, :] += eight_sum(lam * (d_ai * cos - d_ar * sin))
    first = (pl.num_programs(1) - 1 - tile) * tokens
    hit = keep_mask(rel_ref, row, first, (tokens, chan))
    d_f = jnp.where(hit, 0.0, d_lam) * (1.0 - forget)
    dgate_ref[8:16, :] += eight_sum(d_f)
    rest = 1.0 - lam
    d_proj = jnp.concatenate(
        [
            (rest * g_r * (s_r + in_r * (1.0 - s_r))).astype(BF16),
            (rest * g_i * (s_i + in_i * (1.0 - s_i))).astype(BF16),
            (d_f * (1.0 - lower) * forget).astype(BF16),
            dpg_ref[...],
        ],
        axis=1,
    )
    dproj_ref[...] = d_proj
    d_n = dot_t(d_proj, w_ref[...])
    x = x_ref[...].astype(F32)
    scale = rms_scale(x)
    hat = x * scale
    dgain_ref[...] += eight_sum(d_n * hat)
    d_hat = d_n * gain_ref[0:1, :]
    dx_ref[...] = dmid_ref[...] + scale * (d_hat - hat * jnp.mean(d_hat * hat, axis=-1, keepdims=True))


def carry_kernel(axis, count, forward, tot_ref, rot_ref, out_ref, buf, send_sem, recv_sem):
    me = lax.axis_index(axis)
    barrier = pltpu.get_barrier_semaphore()
    peers = [lax.rem(me + k, count) for k in range(1, count)]
    for peer in peers:
        pl.semaphore_signal(barrier, inc=1, device_id={axis: peer}, device_id_type=MESH)
    pl.semaphore_wait(barrier, count - 1)
    copies = []
    for k, peer in enumerate(peers):
        copy = pltpu.make_async_remote_copy(
            src_ref=tot_ref,
            dst_ref=buf.at[k],
            send_sem=send_sem.at[k],
            recv_sem=recv_sem.at[k],
            device_id={axis: peer},
            device_id_type=MESH,
        )
        copy.start()
        copies.append(copy)
    for copy in copies:
        copy.wait()
    cos, sin = rot_ref[0:1, :], rot_ref[1:2, :]
    rows = tot_ref.shape[0]
    for r in range(rows):
        c_r = jnp.zeros_like(cos)
        c_i = jnp.zeros_like(cos)
        for k in range(count - 1, 0, -1):
            slot = k - 1 if forward else count - k - 1
            valid = me >= k if forward else me + k < count
            e_r, e_i, m = buf[slot, r, 0:1, :], buf[slot, r, 1:2, :], buf[slot, r, 2:3, :]
            a_r = m * cos
            a_i = m * sin if forward else -m * sin
            n_r = a_r * c_r - a_i * c_i + e_r
            n_i = a_r * c_i + a_i * c_r + e_i
            keep = jnp.where(valid, 1.0, 0.0)
            c_r, c_i = n_r * keep, n_i * keep
        out_ref[r, 0:1, :] = c_r
        out_ref[r, 1:2, :] = c_i


def vmem(bytes_):
    return pltpu.CompilerParams(vmem_limit_bytes=bytes_)


def whole(*shape):
    return pl.BlockSpec(shape, lambda *_: (0,) * len(shape), pipeline_mode=pl.Buffered(1))


def make_carry(count, rows, chan, forward):
    return pl.pallas_call(
        functools.partial(carry_kernel, "seq", count, forward),
        out_shape=jax.ShapeDtypeStruct((rows, 8, chan), F32),
        in_specs=[pl.BlockSpec(memory_space=pltpu.VMEM)] * 2,
        out_specs=pl.BlockSpec(memory_space=pltpu.VMEM),
        scratch_shapes=[
            pltpu.VMEM((count - 1, rows, 8, chan), F32),
            pltpu.SemaphoreType.DMA((count - 1,)),
            pltpu.SemaphoreType.DMA((count - 1,)),
        ],
        compiler_params=pltpu.CompilerParams(
            collective_id=1 if forward else 2, has_side_effects=True
        ),
    )


LIMIT = 48 * 1024 * 1024


def layer_calls(rows, length, width, hidden, cols, n_seq, tokens):
    chan = width // 2
    tiles = length // tokens
    total = rows * length
    grid = (rows, tiles)
    shape = jax.ShapeDtypeStruct
    smem = pl.BlockSpec(memory_space=pltpu.SMEM)

    def fwd(w, col=0):
        return pl.BlockSpec((tokens, w), lambda r, t: (r * tiles + t, col))

    def fwd_l(w):
        return pl.BlockSpec((w // LANES, tokens, LANES), lambda r, t: (0, r * tiles + t, 0))

    def bwd_l(w):
        return pl.BlockSpec(
            (w // LANES, tokens, LANES), lambda r, t: (0, r * tiles + tiles - 1 - t, 0)
        )

    def split(w):
        return shape((w // LANES, total, LANES), F32)

    def bwd(w, col=0):
        return pl.BlockSpec((tokens, w), lambda r, t: (r * tiles + tiles - 1 - t, col))

    ends_f = pl.BlockSpec((1, 24, chan), lambda r, t: (r * tiles + t, 0, 0))
    ends_b = pl.BlockSpec((1, 24, chan), lambda r, t: (r * tiles + tiles - 1 - t, 0, 0))
    per_row = pl.BlockSpec((1, 8, chan), lambda r, t: (r, 0, 0))
    ends_s = shape((rows * tiles, 24, chan), F32)
    row_s = shape((rows, 8, chan), F32)

    enter = pl.pallas_call(
        enter_kernel,
        grid=grid,
        in_specs=[smem, fwd(width), whole(width, cols), whole(8, width), whole(8, chan)],
        out_specs=[fwd(cols), fwd(width), fwd_l(chan), fwd_l(width), fwd_l(chan), ends_f, per_row],
        out_shape=[
            shape((total, cols), BF16),
            shape((total, width), BF16),
            split(chan),
            split(width),
            split(chan),
            ends_s,
            row_s,
        ],
        scratch_shapes=[pltpu.VMEM((width // LANES, tokens, LANES), F32)],
        compiler_params=vmem(LIMIT),
    )

    def leave(out_type):
        return pl.pallas_call(
            leave_kernel,
            grid=grid,
            in_specs=[
                fwd(width),
                fwd(width),
                fwd_l(width),
                fwd_l(chan),
                ends_f,
                per_row,
                whole(width, width),
                whole(width, 2 * hidden),
                whole(hidden, width),
                whole(8, width),
                whole(8, chan),
            ],
            out_specs=[
                fwd_l(width),
                fwd_l(width),
                fwd(width),
                fwd(width),
                fwd(width),
                fwd(2 * hidden),
                fwd(hidden),
                fwd(width),
            ],
            out_shape=[
                split(width),
                split(width),
                shape((total, width), BF16),
                shape((total, width), F32),
                shape((total, width), BF16),
                shape((total, 2 * hidden), BF16),
                shape((total, hidden), BF16),
                shape((total, width), out_type),
            ],
            scratch_shapes=[pltpu.VMEM((8, chan), F32)],
            compiler_params=vmem(LIMIT),
        )

    back_out = pl.pallas_call(
        back_out_kernel,
        grid=grid,
        in_specs=[
            bwd(width),
            bwd(2 * hidden),
            bwd(width),
            bwd_l(width),
            bwd(width),
            bwd_l(chan),
            whole(width, width),
            whole(width, 2 * hidden),
            whole(hidden, width),
            whole(8, width),
            whole(8, chan),
        ],
        out_specs=[
            bwd(width),
            bwd(2 * hidden),
            bwd(width),
            bwd(width),
            bwd(width),
            bwd_l(width),
            bwd_l(chan),
            ends_b,
            per_row,
            pl.BlockSpec((16, width), lambda r, t: (0, 0)),
        ],
        out_shape=[
            shape((total, width), BF16),
            shape((total, 2 * hidden), BF16),
            shape((total, width), F32),
            shape((total, width), BF16),
            shape((total, width), BF16),
            split(width),
            split(chan),
            ends_s,
            row_s,
            shape((16, width), F32),
        ],
        scratch_shapes=[pltpu.VMEM((width // LANES, tokens, LANES), F32)],
        compiler_params=vmem(LIMIT),
    )

    back_in = pl.pallas_call(
        back_in_kernel,
        grid=grid,
        in_specs=[
            smem,
            bwd(width),
            bwd(width),
            bwd(3 * chan),
            bwd(width),
            bwd_l(chan),
            bwd_l(width),
            bwd_l(width),
            bwd_l(chan),
            ends_b,
            per_row,
            whole(width, cols),
            whole(8, width),
            whole(8, chan),
        ],
        out_specs=[
            bwd(cols),
            bwd(width),
            pl.BlockSpec((8, width), lambda r, t: (0, 0)),
            pl.BlockSpec((16, chan), lambda r, t: (0, 0)),
        ],
        out_shape=[
            shape((total, cols), BF16),
            shape((total, width), F32),
            shape((8, width), F32),
            shape((16, chan), F32),
        ],
        scratch_shapes=[
            pltpu.VMEM((8, chan), F32),
            pltpu.VMEM((width // LANES, tokens, LANES), F32),
        ],
        compiler_params=vmem(LIMIT),
    )
    carry_f = make_carry(n_seq, rows, chan, True)
    carry_b = make_carry(n_seq, rows, chan, False)
    return enter, carry_f, leave, back_out, carry_b, back_in


def contract_rows(left, right):
    return lax.dot_general(
        left, right, (((0,), (0,)), ((), ())), preferred_element_type=F32
    ).astype(BF16)


def shards(
    tokens_in, doc_starts, mixer_in, mixer_out, ffn_in, ffn_out, gains, gate_params, cotangent
):
    rows, length, width = tokens_in.shape
    chan = width // 2
    n_seq = lax.axis_size("seq")
    hidden = ffn_in.shape[2] // 2
    cols = mixer_in.shape[2]
    total = rows * length
    tokens = min(length, 256)
    seg = tokens // 8
    enter, carry_f, leave, back_out, carry_b, back_in = layer_calls(
        rows, length, width, hidden, cols, n_seq, tokens
    )
    rel = doc_starts - lax.axis_index("seq") * length
    gain_rows = jnp.pad(gains, ((0, 0), (0, 5), (0, 0)))
    theta, lower = gate_params[:, 0], gate_params[:, 1]
    gate_rows = jnp.stack(
        [jnp.cos(theta), jnp.sin(theta), lower, jnp.cos(theta * seg), jnp.sin(theta * seg),
         jnp.cos(theta * length), jnp.sin(theta * length), lower], axis=1
    )
    x = tokens_in.reshape(total, width)
    saved = []
    for k in range(LAYERS):
        w_in = lax.all_gather(mixer_in[k], "batch", axis=0, tiled=True)
        w_out = lax.all_gather(mixer_out[k], "batch", axis=0, tiled=True)
        w_ffn = lax.all_gather(ffn_in[k], "batch", axis=0, tiled=True)
        w_down = lax.all_gather(ffn_out[k], "batch", axis=0, tiled=True)
        proj, normed, lam, h, cum, ends, tot = enter(rel, x, w_in, gain_rows[k], gate_rows[k])
        carry = carry_f(tot, gate_rows[k, 5:8])
        state, prior, mixed, mid, normed2, gu, hid, nxt = leave(F32 if k + 1 < LAYERS else BF16)(
            x, proj[:, 3 * chan :], h, cum, ends, carry, w_out, w_ffn, w_down, gain_rows[k], gate_rows[k]
        )
        saved.append((w_in, w_out, w_ffn, w_down, x, proj, normed, lam, state, prior, mixed, mid,
                      normed2, gu, hid))
        x = nxt
    block_out = x.reshape(rows, length, width)
    dx = cotangent.reshape(total, width)
    big, small_gain, small_gate = [None] * LAYERS, [None] * LAYERS, [None] * LAYERS
    for k in reversed(range(LAYERS)):
        (w_in, w_out, w_ffn, w_down, x, proj, normed, lam, state, prior, mixed, mid,
         normed2, gu, hid) = saved[k]
        dz, d_gu, d_mid, dy, d_pg, g, cum, ends, tot, dg_a = back_out(
            dx, gu, mid, state, proj[:, 3 * chan :], lam, w_out, w_ffn, w_down, gain_rows[k], gate_rows[k]
        )
        carry = carry_b(tot, gate_rows[k, 5:8])
        d_proj, dx, dg_b, dgate = back_in(
            rel, x, d_mid, proj, d_pg, lam, prior, g, cum, ends, carry, w_in, gain_rows[k], gate_rows[k]
        )
        big[k] = (
            contract_rows(normed, d_proj),
            contract_rows(mixed, dy),
            contract_rows(normed2, d_gu),
            contract_rows(hid, dz),
        )
        small_gain[k] = jnp.stack(
            [jnp.sum(dg_b, axis=0), jnp.sum(dg_a[:8], axis=0), jnp.sum(dg_a[8:], axis=0)]
        )
        small_gate[k] = jnp.stack([jnp.sum(dgate[:8], axis=0), jnp.sum(dgate[8:], axis=0)])
    d_gains, d_gate_params = lax.psum(
        (jnp.stack(small_gain), jnp.stack(small_gate)), ("batch", "seq")
    )
    outs = []
    for m in range(4):
        parts = []
        for k in range(LAYERS):
            part = lax.psum_scatter(big[k][m], "batch", scatter_dimension=0, tiled=True)
            parts.append(lax.psum(part, "seq").astype(F32))
        outs.append(jnp.stack(parts))
    return (block_out, dx.reshape(rows, length, width), *outs, d_gains, d_gate_params)


def solution(mesh):
    tok = P("batch", "seq", None)
    mat = P(None, "batch", None)
    return jax.shard_map(
        shards,
        mesh=mesh,
        in_specs=(tok, P("batch", None), mat, mat, mat, mat, P(), P(), tok),
        out_specs=(tok, tok, mat, mat, mat, mat, P(), P()),
        check_vma=False,
    )
```

time: 2170 us -> 1260 us (0.58); the launches traced: 2130 us -> 1250 us
  local copies, waits for them, and re-layouts: 1210 us -> 43.1 us
  waiting for transfers between devices: 334 us -> 890 us
  other arithmetic: 324 us -> 7.37 us
  Pallas kernels: 0 us -> 200 us
  matrix products: 166 us -> 49.9 us
  starting transfers between devices: 30.4 us -> 1.08 us
    slice x519 -> x6, local copies, waits for them, and re-layouts: 921 us -> 10.1 us  [the longest x2 4.28 us: shards(): proj[:, 3 * chan:]]
    all_gather x8, waiting for transfers between devices: 53.8 us -> 385 us  [the longest x2 162 us: shards(): w_ffn = lax.all_gather(ffn_in[k], 'batch', axis=0, tiled=True)]
    reduce_scatter x8, waiting for transfers between devices: 194 us -> 478 us  [shards(): part = lax.psum_scatter(big[k][m], 'batch', scatter_dimension=0, tiled=True)]
    pallas_call x0 -> x12, Pallas kernels: none -> 200 us  [the longest x2 60.3 us: shards(): back_out(dx, gu, mid, state, proj[:, 3 * chan:], lam, w_out, w_ffn, w_dow...]
    add x255 -> x0, other arithmetic: 181 us -> none  [the longest x54 75.7 us: complex_combine(): later_term_real * earlier_source_imaginary]
    pad x256 -> x0, local copies, waits for them, and re-layouts: 139 us -> none  [linear_chain(): lax.associative_scan(complex_combine, (decay_r, decay_i, source_r, source...]
    dot_general x16 -> x0, matrix products: 113 us -> none  [the longest x8 61.4 us: contract_cols(): lax.dot_general(left, right, (((1,), (1,)), ((), ())), preferred_element_...]
    rev x10 -> x0, local copies, waits for them, and re-layouts: 98 us -> none  [the longest x2 25.9 us: layer_backward(): back_g_i = rev_g_i[:, ::-1]]
  transfers between devices with their start and end apart: 29 -> 17, of which waited for: 16 -> 15; matrix products, arithmetic and copies ran while one was open for 58% -> 5% of each run, Pallas kernels for 0% -> 12%
where the time goes in v1:
time: 1260 us; the launch traced here: 1250 us
  waiting for transfers between devices  890 us (71%)
  Pallas kernels  200 us (16%)
  matrix products  49.9 us (4%)
  local copies, waits for them, and re-layouts  43.1 us (3%)
  blocking collectives  41.3 us (3%)
  between operations  14.6 us (1%)
    reduce_scatter x8, waiting for transfers between devices, shards(): part = lax.psum_scatter(big[k][m], 'batch', scatter_dimension=0, tiled=True)  478 us
    all_gather x2, waiting for transfers between devices, shards(): w_ffn = lax.all_gather(ffn_in[k], 'batch', axis=0, tiled=True)  162 us
    all_gather x2, waiting for transfers between devices, shards(): w_down = lax.all_gather(ffn_out[k], 'batch', axis=0, tiled=True)  106 us
    all_gather x2, waiting for transfers between devices, shards(): w_in = lax.all_gather(mixer_in[k], 'batch', axis=0, tiled=True)  83.7 us
    pallas_call x2, Pallas kernels, shards(): back_out(dx, gu, mid, state, proj[:, 3 * chan:], lam, w_out, w_ffn, w_dow...  60.3 us
    pallas_call x2, Pallas kernels, shards(): leave(F32 if k + 1 < LAYERS else BF16)  51.3 us
    dot_general x8, matrix products, contract_rows(): lax.dot_general(left, right, (((0,), (0,)), ((), ())), preferred_element_...  49.9 us
    psum x1, blocking collectives, shards(): lax.psum((jnp.stack(small_gain), jnp.stack(small_gate)), ('batch', 'seq'))  41.3 us
  transfers between devices with their start and end apart: 17, of which 15 were waited for; matrix products, arithmetic and copies ran while one was open for 5% of the time, Pallas kernels for 12%

profile of v1, /device:TPU:0, one launch (start us, length us, event | category | flops | bytes accessed | tf_op | source)
XLA Modules:
  0.0 1247.7 jit_solution(4724880416661649584)
XLA Ops:
  17.1 54.8 %all-gather.17.cloned.1.call-done = bf16[1,768,1920]{2,1,0:T(8,128)(2,1)} async-done(((bf16[1,96,1920]{2,1,0:T(8,128)(2,1)}), bf16[1,768,1920]{2,1,0:T(8,128)(2,1)}) %all-gather.17.cloned.1.call-update) | async-done | bytes 2949136 | tf_op jit(solution)/shard_map/all_gather | solution.py:635
  71.9 14.0 %shard_map.152 = (bf16[1024,1920]{1,0:T(8,128)(2,1)}, bf16[1024,768]{1,0:T(8,128)(2,1)S(1)}, f32[3,1024,128]{2,1,0:T(8,128)S(1)}, f32[6,1024,128]{2,1,0:T(8,128)...) custom-call(s32[2,6]{1,0:T(2,128)S(1)} %broadcast_subtract_fusion.rel_ref, ...), custom_call_target="tpu_custom_call" | custom-call | tf_op jit(solution)/shard_map/pallas_call | solution.py:639
  98.0 15.8 %all-gather.19.cloned.1.call-done = bf16[1,768,768]{2,1,0:T(8,128)(2,1)} async-done(((bf16[1,96,768]{2,1,0:T(8,128)(2,1)}), bf16[1,768,768]{2,1,0:T(8,128)(2,1)}) %all-gather.19.cloned.1.call-update) | async-done | bytes 1179664 | tf_op jit(solution)/shard_map/all_gather | solution.py:636
  113.8 53.1 %all-gather.23.cloned.1.call-done = bf16[1,1536,768]{2,1,0:T(8,128)(2,1)} async-done(((bf16[1,192,768]{2,1,0:T(8,128)(2,1)}), bf16[1,1536,768]{2,1,0:T(8,128)(2,1)}) %all-gather.23.cloned.1.call-update) | async-done | bytes 2359312 | tf_op jit(solution)/shard_map/all_gather | solution.py:638
  166.9 81.1 %all-gather.21.cloned.1.call-done = bf16[1,768,3072]{2,1,0:T(8,128)(2,1)} async-done(((bf16[1,96,3072]{2,1,0:T(8,128)(2,1)}), bf16[1,768,3072]{2,1,0:T(8,128)(2,1)}) %all-gather.21.cloned.1.call-update) | async-done | bytes 4718608 | tf_op jit(solution)/shard_map/all_gather | solution.py:637
  249.9 25.7 %shard_map.154 = (f32[6,1024,128]{2,1,0:T(8,128)}, f32[6,1024,128]{2,1,0:T(8,128)}, bf16[1024,768]{1,0:T(8,128)(2,1)S(1)}, f32[1024,768]{1,0:T(8,128)}, bf16[102...) custom-call(bf16[1024,768]{1,0:T(8,128)(2,1)S(1)} %bitcast.57, ...), custom_call_target="tpu_custom_call" | custom-call | tf_op jit(solution)/shard_map/pallas_call | solution.py:641
  277.9 28.9 %all-gather.25.cloned.1.call-done = bf16[1,768,1920]{2,1,0:T(8,128)(2,1)} async-done(((bf16[1,96,1920]{2,1,0:T(8,128)(2,1)}), bf16[1,768,1920]{2,1,0:T(8,128)(2,1)}) %all-gather.25.cloned.1.call-update) | async-done | bytes 2949136 | tf_op jit(solution)/shard_map/all_gather | solution.py:635
  306.8 14.0 %shard_map.155 = (bf16[1024,1920]{1,0:T(8,128)(2,1)}, bf16[1024,768]{1,0:T(8,128)(2,1)S(1)}, f32[3,1024,128]{2,1,0:T(8,128)S(1)}, f32[6,1024,128]{2,1,0:T(8,128)...) custom-call(s32[2,6]{1,0:T(2,128)S(1)} %broadcast_subtract_fusion.rel_ref, ...), custom_call_target="tpu_custom_call" | custom-call | tf_op jit(solution)/shard_map/pallas_call | solution.py:639
  331.8 16.8 %all-gather.27.cloned.1.call-done = bf16[1,768,768]{2,1,0:T(8,128)(2,1)} async-done(((bf16[1,96,768]{2,1,0:T(8,128)(2,1)}), bf16[1,768,768]{2,1,0:T(8,128)(2,1)}) %all-gather.27.cloned.1.call-update) | async-done | bytes 1179664 | tf_op jit(solution)/shard_map/all_gather | solution.py:636
  348.6 53.1 %all-gather.31.cloned.1.call-done = bf16[1,1536,768]{2,1,0:T(8,128)(2,1)} async-done(((bf16[1,192,768]{2,1,0:T(8,128)(2,1)}), bf16[1,1536,768]{2,1,0:T(8,128)(2,1)}) %all-gather.31.cloned.1.call-update) | async-done | bytes 2359312 | tf_op jit(solution)/shard_map/all_gather | solution.py:638
  401.6 81.2 %all-gather.29.cloned.1.call-done = bf16[1,768,3072]{2,1,0:T(8,128)(2,1)} async-done(((bf16[1,96,3072]{2,1,0:T(8,128)(2,1)}), bf16[1,768,3072]{2,1,0:T(8,128)(2,1)}) %all-gather.29.cloned.1.call-update) | async-done | bytes 4718608 | tf_op jit(solution)/shard_map/all_gather | solution.py:637
  484.9 25.6 %shard_map.157 = (f32[6,1024,128]{2,1,0:T(8,128)}, f32[6,1024,128]{2,1,0:T(8,128)}, bf16[1024,768]{1,0:T(8,128)(2,1)S(1)}, f32[1024,768]{1,0:T(8,128)}, bf16[102...) custom-call(f32[1024,768]{1,0:T(8,128)} %get-tuple-element.71.x_ref,, ...), custom_call_target="tpu_custom_call" | custom-call | tf_op jit(solution)/shard_map/pallas_call | solution.py:641
  511.6 30.2 %shard_map.158 = (bf16[1024,768]{1,0:T(8,128)(2,1)S(1)}, bf16[1024,3072]{1,0:T(8,128)(2,1)}, f32[1024,768]{1,0:T(8,128)}, bf16[1024,768]{1,0:T(8,128)(2,1)S(1)},...) custom-call(bf16[1024,768]{1,0:T(8,128)(2,1)} %bitcast.75, ...), custom_call_target="tpu_custom_call" | custom-call | tf_op jit(solution)/shard_map/pallas_call | solution.py:653
  555.6 19.7 %shard_map.160 = (bf16[1024,1920]{1,0:T(8,128)(2,1)}, f32[1024,768]{1,0:T(8,128)}, f32[8,768]{1,0:T(8,128)S(1)}, f32[16,384]{1,0:T(8,128)S(1)}) custom-call(s32[2,6]{1,0:T(2,128)S(1)} %broadcast_subtract_fusion.rel_ref, f32[1024,768]{1,0:T(8,128)} %get-tuple-element.71.x_ref, f32[1024,768]{1,0:T(8,128)} %get-tuple-element.82.dmid_ref, ...), custom_call_target="tpu_custom_call" | custom-call | tf_op jit(solution)/shard_map/pallas_call | solution.py:657
  575.3 30.1 %shard_map.161 = (bf16[1024,768]{1,0:T(8,128)(2,1)S(1)}, bf16[1024,3072]{1,0:T(8,128)(2,1)}, f32[1024,768]{1,0:T(8,128)}, bf16[1024,768]{1,0:T(8,128)(2,1)S(1)},...) custom-call(f32[1024,768]{1,0:T(8,128)} %get-tuple-element.89.dx_ref, ...), custom_call_target="tpu_custom_call" | custom-call | tf_op jit(solution)/shard_map/pallas_call | solution.py:653
  631.2 19.4 %shard_map.163 = (bf16[1024,1920]{1,0:T(8,128)(2,1)}, f32[1024,768]{1,0:T(8,128)}, f32[8,768]{1,0:T(8,128)S(1)}, f32[16,384]{1,0:T(8,128)S(1)}) custom-call(s32[2,6]{1,0:T(2,128)S(1)} %broadcast_subtract_fusion.rel_ref, bf16[1024,768]{1,0:T(8,128)(2,1)S(1)} %bitcast.58, f32[1024,768]{1,0:T(8,128)} %get-tuple-element.94.dmid_ref, ...), custom_call_target="tpu_custom_call" | custom-call | tf_op jit(solution)/shard_map/pallas_call | solution.py:657
  688.6 59.5 %reduce-scatter.23.cloned.1.call-done = bf16[192,768]{1,0:T(8,128)(2,1)} async-done(((bf16[1536,768]{1,0:T(8,128)(2,1)}), bf16[192,768]{1,0:T(8,128)(2,1)}) %reduce-scatter.23.cloned.1.call-update) | async-done | bytes 294928 | tf_op jit(solution)/shard_map/reduce_scatter | solution.py:677
  748.1 71.5 %reduce-scatter.21.cloned.1.call-done = bf16[192,768]{1,0:T(8,128)(2,1)} async-done(((bf16[1536,768]{1,0:T(8,128)(2,1)}), bf16[192,768]{1,0:T(8,128)(2,1)}) %reduce-scatter.21.cloned.1.call-update) | async-done | bytes 294928 | tf_op jit(solution)/shard_map/reduce_scatter | solution.py:677
  819.5 75.1 %reduce-scatter.9.cloned.1.call-done = bf16[96,1920]{1,0:T(8,128)(2,1)} async-done(((bf16[768,1920]{1,0:T(8,128)(2,1)}), bf16[96,1920]{1,0:T(8,128)(2,1)}) %reduce-scatter.9.cloned.1.call-update) | async-done | bytes 368656 | tf_op jit(solution)/shard_map/reduce_scatter | solution.py:677
  894.6 75.7 %reduce-scatter.11.cloned.1.call-done = bf16[96,1920]{1,0:T(8,128)(2,1)} async-done(((bf16[768,1920]{1,0:T(8,128)(2,1)}), bf16[96,1920]{1,0:T(8,128)(2,1)}) %reduce-scatter.11.cloned.1.call-update) | async-done | bytes 368656 | tf_op jit(solution)/shard_map/reduce_scatter | solution.py:677
  970.3 98.1 %reduce-scatter.17.cloned.1.call-done = bf16[96,3072]{1,0:T(8,128)(2,1)} async-done(((bf16[768,3072]{1,0:T(8,128)(2,1)}), bf16[96,3072]{1,0:T(8,128)(2,1)}) %reduce-scatter.17.cloned.1.call-update) | async-done | bytes 589840 | tf_op jit(solution)/shard_map/reduce_scatter | solution.py:677
  1068.3 98.5 %reduce-scatter.19.cloned.1.call-done = bf16[96,3072]{1,0:T(8,128)(2,1)} async-done(((bf16[768,3072]{1,0:T(8,128)(2,1)}), bf16[96,3072]{1,0:T(8,128)(2,1)}) %reduce-scatter.19.cloned.1.call-update) | async-done | bytes 589840 | tf_op jit(solution)/shard_map/reduce_scatter | solution.py:677
  1167.3 41.3 %all-reduce.1 = (f32[2,3,768]{2,1,0:T(4,128)S(1)}, f32[2,2,384]{2,1,0:T(2,128)}) all-reduce(f32[2,3,768]{2,1,0:T(4,128)S(1)} %pad_maximum_fusion, f32[2,2,384]{2,1,0:T(2,128)S(1)} %pad_maximum_fusion.2), channel_id=1, replica_groups=mesh['batch'=8,'seq'=4] {'batch','seq'}, use_global_device_ids=true, to_apply=%region_22.23 | all-reduce | flops 6144 | bytes 49152 | tf_op jit(solution)/shard_map/psum | solution.py:670
  1209.2 24.8 %all-reduce.5.cloned.1.call-done = (bf16[1,96,1920]{2,1,0:T(8,128)(2,1)}, bf16[1,96,1920]{2,1,0:T(8,128)(2,1)}, bf16[1,96,768]{2,1,0:T(8,128)(2,1)}, bf16[1,96,7...) async-done(((bf16[1,96,1920]{2,1,0:T(8,128)(2,1)}, ...) | async-done | bytes 2801680 | tf_op jit(solution)/shard_map/psum | solution.py:678
  (187 shorter events, 125.3 us)
Async XLA Ops:
  7.2 64.7 %all-gather.17.cloned.1.call-start = ((), (), s32[]{:S(2)}) async-start(), calls=%async_computation.16 | async-start | bytes 3317760 | tf_op jit(solution)/shard_map/all_gather | solution.py:635
  9.4 104.4 %all-gather.19.cloned.1.call-start = ((), (), s32[]{:S(2)}) async-start(), calls=%async_computation.17 | async-start | bytes 1327104 | tf_op jit(solution)/shard_map/all_gather | solution.py:636
  11.2 155.7 %all-gather.23.cloned.1.call-start = ((), (), s32[]{:S(2)}) async-start(), calls=%async_computation.19 | async-start | bytes 2654208 | tf_op jit(solution)/shard_map/all_gather | solution.py:638
  12.1 235.8 %all-gather.21.cloned.1.call-start = ((), (), s32[]{:S(2)}) async-start(), calls=%async_computation.18 | async-start | bytes 5308416 | tf_op jit(solution)/shard_map/all_gather | solution.py:637
  13.3 293.5 %all-gather.25.cloned.1.call-start = ((), (), s32[]{:S(2)}) async-start(), calls=%async_computation.20 | async-start | bytes 3317760 | tf_op jit(solution)/shard_map/all_gather | solution.py:635
  13.9 334.7 %all-gather.27.cloned.1.call-start = ((), (), s32[]{:S(2)}) async-start(), calls=%async_computation.21 | async-start | bytes 1327104 | tf_op jit(solution)/shard_map/all_gather | solution.py:636
  14.5 387.2 %all-gather.31.cloned.1.call-start = ((), (), s32[]{:S(2)}) async-start(), calls=%async_computation.23 | async-start | bytes 2654208 | tf_op jit(solution)/shard_map/all_gather | solution.py:638
  15.2 467.6 %all-gather.29.cloned.1.call-start = ((), (), s32[]{:S(2)}) async-start(), calls=%async_computation.22 | async-start | bytes 5308416 | tf_op jit(solution)/shard_map/all_gather | solution.py:637
  16.0 672.6 %reduce-scatter.15.cloned.1.call-start = ((), (), s32[]{:S(2)}) async-start(), calls=%async_computation.11 | async-start | bytes 1327104 | tf_op jit(solution)/shard_map/reduce_scatter | solution.py:677
  90.0 157.9 %copy-start = (bf16[2,512,768]{2,1,0:T(8,128)(2,1)S(1)}, bf16[2,512,768]{2,1,0:T(8,128)(2,1)}, u32[]{:S(2)}) copy-start(bf16[2,512,768]{2,1,0:T(8,128)(2,1)} %param.9) | copy-start | bytes 4718596
  326.5 184.0 %copy-start.1 = (bf16[1024,768]{1,0:T(8,128)(2,1)}, bf16[1024,768]{1,0:T(8,128)(2,1)S(1)}, u32[]{:S(2)}) copy-start(bf16[1024,768]{1,0:T(8,128)(2,1)S(1)} %slice.109.proj_ref) | copy-start | bytes 4718596
  484.9 26.8 %copy-start.9 = (bf16[1,768,768]{2,1,0:T(8,128)(2,1)S(1)}, bf16[1,768,768]{2,1,0:T(8,128)(2,1)}, u32[]{:S(2)}) copy-start(bf16[1,768,768]{2,1,0:T(8,128)(2,1)} %all-gather.27.cloned.1.call-done) | copy-start | bytes 3538948
  546.7 141.9 %reduce-scatter.13.cloned.1.call-start = ((), (), s32[]{:S(2)}) async-start(), calls=%async_computation.10 | async-start | bytes 1327104 | tf_op jit(solution)/shard_map/reduce_scatter | solution.py:677
  555.6 19.7 %copy-start.7 = (bf16[1,768,768]{2,1,0:T(8,128)(2,1)S(1)}, bf16[1,768,768]{2,1,0:T(8,128)(2,1)}, u32[]{:S(2)}) copy-start(bf16[1,768,768]{2,1,0:T(8,128)(2,1)} %all-gather.19.cloned.1.call-done) | copy-start | bytes 3538948
  575.3 32.4 %copy-start.36 = (bf16[1024,768]{1,0:T(8,128)(2,1)S(1)}, bf16[1024,768]{1,0:T(8,128)(2,1)}, u32[]{:S(2)}) copy-start(bf16[1024,768]{1,0:T(8,128)(2,1)} %copy-done.35) | copy-start | bytes 4718596
  610.2 137.9 %reduce-scatter.23.cloned.1.call-start = ((), (), s32[]{:S(2)}) async-start(), calls=%async_computation.15 | async-start | bytes 2654208 | tf_op jit(solution)/shard_map/reduce_scatter | solution.py:677
  616.2 203.3 %reduce-scatter.21.cloned.1.call-start = ((), (), s32[]{:S(2)}) async-start(), calls=%async_computation.14 | async-start | bytes 2654208 | tf_op jit(solution)/shard_map/reduce_scatter | solution.py:677
  623.7 270.9 %reduce-scatter.9.cloned.1.call-start = ((), (), s32[]{:S(2)}) async-start(), calls=%async_computation.8 | async-start | bytes 3317760 | tf_op jit(solution)/shard_map/reduce_scatter | solution.py:677
  631.2 20.0 %copy-start.30 = (bf16[1024,768]{1,0:T(8,128)(2,1)S(1)}, bf16[1024,768]{1,0:T(8,128)(2,1)}, u32[]{:S(2)}) copy-start(bf16[1024,768]{1,0:T(8,128)(2,1)} %copy-done.29) | copy-start | bytes 4718596
  658.1 312.1 %reduce-scatter.11.cloned.1.call-start = ((), (), s32[]{:S(2)}) async-start(), calls=%async_computation.9 | async-start | bytes 3317760 | tf_op jit(solution)/shard_map/reduce_scatter | solution.py:677
  666.5 401.8 %reduce-scatter.17.cloned.1.call-start = ((), (), s32[]{:S(2)}) async-start(), calls=%async_computation.12 | async-start | bytes 5308416 | tf_op jit(solution)/shard_map/reduce_scatter | solution.py:677
  677.5 489.4 %reduce-scatter.19.cloned.1.call-start = ((), (), s32[]{:S(2)}) async-start(), calls=%async_computation.13 | async-start | bytes 5308416 | tf_op jit(solution)/shard_map/reduce_scatter | solution.py:677
  688.5 478.6 %copy-start.26 = (f32[8,768]{1,0:T(8,128)S(1)}, f32[8,768]{1,0:T(8,128)}, u32[]{:S(2)}) copy-start(f32[8,768]{1,0:T(8,128)} %copy-done.25) | copy-start | bytes 73732
  688.5 545.5 %all-reduce.5.cloned.1.call-start = ((), (), s32[]{:S(2)}) async-start(), calls=%async_computation.24 | async-start | bytes 5603328 | tf_op jit(solution)/shard_map/psum | solution.py:678
  (43 other events, 93.6 us)
Sparse Core Ops, SparseCore 0:
  10.8 61.0 all-gather.16
  74.1 39.6 all-gather.18
  116.0 50.8 all-gather.22
  169.5 78.4 all-gather.20
  250.5 56.2 all-gather.24
  308.9 39.6 all-gather.26
  350.8 50.8 all-gather.30
  404.4 78.4 all-gather.28
  546.8 62.3 reduce-scatter.14
  613.0 63.0 reduce-scatter.12
  680.2 67.8 reduce-scatter.22
  751.4 68.0 reduce-scatter.20
  823.1 71.4 reduce-scatter.8
  898.4 71.7 reduce-scatter.10
  973.8 94.5 reduce-scatter.16
  1071.8 95.0 reduce-scatter.18
  1169.6 64.3 all-reduce.4

commit v2 on v1

--- a/solution.py
+++ b/solution.py
@@ -396,6 +396,309 @@
             c_r, c_i = n_r * keep, n_i * keep
         out_ref[r, 0:1, :] = c_r
         out_ref[r, 1:2, :] = c_i
+
+
+class Ring:
+    def __init__(self, n):
+        self.n = n
+        self.batch, self.seq = lax.axis_index("batch"), lax.axis_index("seq")
+        z, x = self.batch // 2, self.batch % 2
+        self.pos = z + x * (n - 1 - 2 * z)
+        self.core, self.y = self.seq % 2, self.seq // 2
+        self.sign = 1 - 2 * self.core
+        self.core_peer = self.seq + self.sign
+        self.y_peer = self.seq + 2 * (1 - 2 * self.y)
+
+    def at(self, distance):
+        p = (self.pos + distance + 2 * self.n) % self.n
+        h = p // (self.n // 2)
+        return 2 * (p + h * (self.n - 1 - 2 * p)) + h
+
+    def ahead(self, hops):
+        return self.at(self.sign * hops)
+
+
+def remote(src, dst, send, recv, device):
+    return pltpu.make_async_remote_copy(
+        src_ref=src, dst_ref=dst, send_sem=send, recv_sem=recv, device_id=device, device_id_type=MESH
+    )
+
+
+def meet(devices):
+    barrier = pltpu.get_barrier_semaphore()
+    for device in devices:
+        pl.semaphore_signal(barrier, inc=1, device_id=device, device_id_type=MESH)
+    pl.semaphore_wait(barrier, len(devices))
+
+
+def gather_kernel(n, layers, mats, *refs):
+    srcs, dsts = refs[:mats], refs[mats : mats + layers * mats]
+    own_sem, ring_send, ring_recv, y_send, y_recv, core_send, core_recv = refs[mats + layers * mats :]
+    ring = Ring(n)
+    far, near = n // 2, n - 1 - n // 2
+    meet([{"batch": ring.ahead(1)}, {"batch": ring.ahead(-1)}, {"seq": ring.y_peer}, {"seq": ring.core_peer}])
+    jobs = []
+    for k in range(layers):
+        for m in range(mats):
+            jobs.append((srcs[m].at[k], dsts[k * mats + m], srcs[m].shape[1] // 6))
+
+    def rows_of(u):
+        base = ring.core * (3 * u)
+        mine = pl.ds(pl.multiple_of(base + ring.y * u, 16), 2 * u)
+        give = pl.ds(pl.multiple_of(base + ring.y * (2 * u), 16), u)
+        take = pl.ds(pl.multiple_of(base + (1 - ring.y) * (2 * u), 16), u)
+        return mine, give, take
+
+    owns = []
+    for j, (src, dst, u) in enumerate(jobs):
+        mine, give, take = rows_of(u)
+        for way, hops in ((1, far), (-1, near)):
+            slot = 0 if way == 1 else far
+            remote(
+                src.at[mine], dst.at[ring.batch, mine], ring_send.at[j], ring_recv.at[j, slot],
+                {"batch": ring.ahead(way)},
+            ).start()
+        own = pltpu.make_async_copy(src, dst.at[ring.batch], own_sem.at[j])
+        own.start()
+        owns.append(own)
+
+    def arrived(j, way, h):
+        src, dst, u = jobs[j]
+        mine, give, take = rows_of(u)
+        hops = far if way == 1 else near
+        slot = h if way == 1 else far + h
+        origin = ring.ahead(-way * (h + 1))
+        piece = dst.at[origin, mine]
+        remote(piece, piece, ring_send.at[j], ring_recv.at[j, slot], {"batch": ring.ahead(way)}).wait_recv()
+        if h + 1 < hops:
+            remote(piece, piece, ring_send.at[j], ring_recv.at[j, slot + 1], {"batch": ring.ahead(way)}).start()
+        half = dst.at[origin, give]
+        remote(half, half, y_send.at[j], y_recv.at[j, slot], {"seq": ring.y_peer}).start()
+        remote(piece, piece, core_send.at[j], core_recv.at[j], {"seq": ring.core_peer}).start()
+
+    def crossed(j, way, h):
+        src, dst, u = jobs[j]
+        mine, give, take = rows_of(u)
+        slot = h if way == 1 else far + h
+        origin = ring.ahead(-way * (h + 1))
+        half = dst.at[origin, take]
+        remote(half, half, y_send.at[j], y_recv.at[j, slot], {"seq": ring.y_peer}).wait_recv()
+        remote(half, half, core_send.at[j], core_recv.at[j], {"seq": ring.core_peer}).start()
+
+    for h in range(far + 1):
+        for j in range(len(jobs)):
+            for way, hops in ((1, far), (-1, near)):
+                if h < hops:
+                    arrived(j, way, h)
+                if 0 <= h - 1 < hops:
+                    crossed(j, way, h - 1)
+    for j, (src, dst, u) in enumerate(jobs):
+        owns[j].wait()
+        for rows, send in ((2 * u, ring_send), (u, y_send), (3 * u, core_send)):
+            view = dst.at[0 : n - 1, 0:rows]
+            remote(view, view, send.at[j], core_recv.at[j], {"seq": ring.core_peer}).wait_send()
+        view = dst.at[0 : n - 1, 0 : 3 * u]
+        remote(view, view, core_send.at[j], core_recv.at[j], {"seq": ring.core_peer}).wait_recv()
+
+
+def gather(n, *srcs):
+    layers = srcs[0].shape[0]
+    mats = len(srcs)
+    jobs = layers * mats
+    any_ = pl.BlockSpec(memory_space=pl.ANY)
+    dma = pltpu.SemaphoreType.DMA
+    outs = pl.pallas_call(
+        functools.partial(gather_kernel, n, layers, mats),
+        out_shape=[jax.ShapeDtypeStruct((n,) + s.shape[1:], BF16) for _ in range(layers) for s in srcs],
+        in_specs=[any_] * mats,
+        out_specs=[any_] * jobs,
+        scratch_shapes=[dma((jobs,)), dma((jobs,)), dma((jobs, n - 1)), dma((jobs,)), dma((jobs, n - 1)),
+                        dma((jobs,)), dma((jobs,))],
+        compiler_params=pltpu.CompilerParams(collective_id=3, has_side_effects=True),
+    )(*srcs)
+    return [o.reshape(n * o.shape[1], o.shape[2]) for o in outs]
+
+
+def add_rows(dst, dst_row, parts, rows):
+    def block(i, _):
+        step = pl.multiple_of(i * 16, 16)
+        total = None
+        for ref, first in parts:
+            value = ref[pl.ds(pl.multiple_of(first + step, 16), 16), :].astype(F32)
+            total = value if total is None else total + value
+        dst[pl.ds(pl.multiple_of(dst_row + step, 16), 16), :] = total.astype(dst.dtype)
+        return 0
+
+    lax.fori_loop(0, rows // 16, block, 0)
+
+
+def scatter_kernel(n, mats, *refs):
+    grads, small = refs[:mats], refs[mats]
+    outs, small_out = refs[mats + 1 : 2 * mats + 1], refs[2 * mats + 1]
+    rest = refs[2 * mats + 2 :]
+    core_buf, y_out, y_buf, ring_out, ring_buf = (rest[i * mats : (i + 1) * mats] for i in range(5))
+    fin, fin_buf, half, half_buf = (rest[(5 + i) * mats : (6 + i) * mats] for i in range(4))
+    small_buf, core_send, core_recv, y_send, y_recv, ring_send, ring_recv, end_send, end_recv, small_send, small_recv = rest[9 * mats :]
+    ring = Ring(n)
+    far, near = n // 2, n - 1 - n // 2
+    core_dev, y_dev = {"seq": ring.core_peer}, {"seq": ring.y_peer}
+    rounds = [core_dev, y_dev]
+    d = 1
+    while d < n:
+        rounds.append({"batch": ring.batch + d * (1 - 2 * ((ring.batch // d) % 2))})
+        d *= 2
+    meet([{"batch": ring.ahead(1)}, {"batch": ring.ahead(-1)}] + rounds)
+    us = [g.shape[1] // 6 for g in grads]
+
+    order = []
+    for h in range(far):
+        order.append((1, h, far - h))
+        if h < near:
+            order.append((-1, h, near - h))
+    order.append((0, 0, 0))
+
+    def core_copy(m, slot, piece):
+        u = us[m]
+        return remote(
+            grads[m].at[piece, pl.ds(pl.multiple_of((1 - ring.core) * (3 * u), 16), 3 * u)],
+            core_buf[m].at[slot], core_send.at[m], core_recv.at[m, slot], core_dev,
+        )
+
+    def y_copy(m, slot):
+        return remote(y_out[m].at[slot], y_buf[m].at[slot], y_send.at[m], y_recv.at[m, slot], y_dev)
+
+    def ring_copy(m, slot, way):
+        return remote(ring_out[m].at[slot], ring_buf[m].at[slot], ring_send.at[m], ring_recv.at[m, slot],
+                      {"batch": ring.ahead(way)})
+
+    for slot, (way, h, dist) in enumerate(order):
+        for m in range(mats):
+            core_copy(m, slot, ring.ahead(-way * dist)).start()
+    small_buf[0] = small[...]
+
+    def small_round(r):
+        return remote(small_buf.at[2 * r], small_buf.at[2 * r + 1], small_send.at[r], small_recv.at[r], rounds[r])
+
+    small_round(0).start()
+
+    def cross(slot):
+        way, h, dist = order[slot]
+        piece = ring.ahead(way * dist)
+        for m in range(mats):
+            u = us[m]
+            core_copy(m, slot, piece).wait_recv()
+            give = 2 * (1 - ring.y) * u
+            add_rows(y_out[m].at[slot], 0, [(grads[m].at[piece], ring.core * (3 * u) + give),
+                                            (core_buf[m].at[slot], give)], u)
+            y_copy(m, slot).start()
+
+    def hop(slot):
+        way, h, dist = order[slot]
+        piece = ring.ahead(way * dist)
+        for m in range(mats):
+            u = us[m]
+            y_copy(m, slot).wait_recv()
+            extra = []
+            if way == 0:
+                prior = [i for i, o in enumerate(order) if o[2] == 1]
+            elif h:
+                prior = [i for i, o in enumerate(order) if o[0] == way and o[1] == h - 1]
+            else:
+                prior = []
+            for i in prior:
+                ring_copy(m, i, order[i][0]).wait_recv()
+            target = fin[m] if way == 0 else ring_out[m].at[slot]
+            own = ring.y * u
+            rest_ = (1 - ring.y) * u
+            base = [(grads[m].at[piece], ring.core * (3 * u) + ring.y * u), (core_buf[m].at[slot], ring.y * u)]
+            more = [(ring_buf[m].at[i], 0) for i in prior]
+            shift = lambda parts, by: [(r, f + by) for r, f in parts]
+            add_rows(target, own, shift(base + more, own) + [(y_buf[m].at[slot], 0)], u)
+            add_rows(target, rest_, shift(base + more, rest_), u)
+            if way:
+                ring_copy(m, slot, way).start()
+
+    def end_copy(m, kind):
+        src, dst, device = ((fin[m], fin_buf[m], y_dev), (half[m], half_buf[m], core_dev))[kind]
+        return remote(src, dst, end_send.at[m, kind], end_recv.at[m, kind], device)
+
+    last = len(order)
+    small_at = 0
+    for t in range(last + 1):
+        if t < last:
+            cross(t)
+        if t >= 1:
+            hop(t - 1)
+        if t >= 1 and small_at < len(rounds):
+            small_round(small_at).wait_recv()
+            total = small_buf[2 * small_at] + small_buf[2 * small_at + 1]
+            small_at += 1
+            if small_at < len(rounds):
+                small_buf[2 * small_at] = total
+                small_round(small_at).start()
+            else:
+                small_out[...] = total
+    for m in range(mats):
+        end_copy(m, 0).start()
+    for m in range(mats):
+        u = us[m]
+        y = ring.y
+        end_copy(m, 0).wait_recv()
+        add_rows(half[m], 2 * y * u, [(fin[m], y * u)], u)
+        add_rows(half[m], 2 * (1 - y) * u, [(fin_buf[m], (1 - y) * u)], u)
+        add_rows(half[m], u, [(fin[m], (1 - y) * u), (fin_buf[m], y * u)], u)
+        end_copy(m, 1).start()
+        add_rows(outs[m], ring.core * (3 * u), [(half[m], 0)], 3 * u)
+    for m in range(mats):
+        u = us[m]
+        end_copy(m, 1).wait_recv()
+        add_rows(outs[m], (1 - ring.core) * (3 * u), [(half_buf[m], 0)], 3 * u)
+    for m in range(mats):
+        end_copy(m, 0).wait_send()
+        end_copy(m, 1).wait_send()
+        remote(core_buf[m], core_buf[m], core_send.at[m], core_recv.at[m, 0], core_dev).wait_send()
+        remote(y_out[m], y_buf[m], y_send.at[m], y_recv.at[m, 0], y_dev).wait_send()
+        remote(ring_out[m], ring_buf[m], ring_send.at[m], ring_recv.at[m, 0], core_dev).wait_send()
+    for r in range(len(rounds)):
+        small_round(r).wait_send()
+
+
+def scatter(n, grads, small):
+    mats = len(grads)
+    grads = [g.reshape(n, g.shape[0] // n, g.shape[1]) for g in grads]
+    us = [(g.shape[1] // 6, g.shape[2]) for g in grads]
+    dma = pltpu.SemaphoreType.DMA
+    vm = pl.BlockSpec(memory_space=pltpu.VMEM)
+    rounds = 2 + (n - 1).bit_length()
+
+    def bufs(f):
+        return [pltpu.VMEM(f(u, w), BF16) for u, w in us]
+
+    outs = pl.pallas_call(
+        functools.partial(scatter_kernel, n, mats),
+        out_shape=[jax.ShapeDtypeStruct(g.shape[1:], F32) for g in grads]
+        + [jax.ShapeDtypeStruct(small.shape, F32)],
+        in_specs=[vm] * (mats + 1),
+        out_specs=[vm] * (mats + 1),
+        scratch_shapes=bufs(lambda u, w: (n, 3 * u, w))
+        + bufs(lambda u, w: (n, u, w))
+        + bufs(lambda u, w: (n, u, w))
+        + bufs(lambda u, w: (n - 1, 2 * u, w))
+        + bufs(lambda u, w: (n - 1, 2 * u, w))
+        + bufs(lambda u, w: (2 * u, w))
+        + bufs(lambda u, w: (2 * u, w))
+        + bufs(lambda u, w: (3 * u, w))
+        + bufs(lambda u, w: (3 * u, w))
+        + [
+            pltpu.VMEM((2 * rounds,) + small.shape, F32),
+            dma((mats,)), dma((mats, n)), dma((mats,)), dma((mats, n)), dma((mats,)), dma((mats, n)),
+            dma((mats, 2)), dma((mats, 2)), dma((rounds,)), dma((rounds,)),
+        ],
+        compiler_params=pltpu.CompilerParams(
+            collective_id=4, has_side_effects=True, vmem_limit_bytes=52 * 1024 * 1024
+        ),
+    )(*grads, small)
+    return outs[:-1], outs[-1]
 
 
 def vmem(bytes_):
@@ -629,13 +932,21 @@
         [jnp.cos(theta), jnp.sin(theta), lower, jnp.cos(theta * seg), jnp.sin(theta * seg),
          jnp.cos(theta * length), jnp.sin(theta * length), lower], axis=1
     )
+    n = lax.axis_size("batch")
+    paired = n_seq == 4 and n % 4 == 0 and all(
+        w.shape[1] % 96 == 0 for w in (mixer_in, mixer_out, ffn_in, ffn_out)
+    )
+    sources = (mixer_in, mixer_out, ffn_in, ffn_out)
+    if paired:
+        gathered = gather(n, *sources)
+    else:
+        gathered = [
+            lax.all_gather(w[k], "batch", axis=0, tiled=True) for k in range(LAYERS) for w in sources
+        ]
     x = tokens_in.reshape(total, width)
     saved = []
     for k in range(LAYERS):
-        w_in = lax.all_gather(mixer_in[k], "batch", axis=0, tiled=True)
-        w_out = lax.all_gather(mixer_out[k], "batch", axis=0, tiled=True)
-        w_ffn = lax.all_gather(ffn_in[k], "batch", axis=0, tiled=True)
-        w_down = lax.all_gather(ffn_out[k], "batch", axis=0, tiled=True)
+        w_in, w_out, w_ffn, w_down = gathered[4 * k : 4 * k + 4]
         proj, normed, lam, h, cum, ends, tot = enter(rel, x, w_in, gain_rows[k], gate_rows[k])
         carry = carry_f(tot, gate_rows[k, 5:8])
         state, prior, mixed, mid, normed2, gu, hid, nxt = leave(F32 if k + 1 < LAYERS else BF16)(
@@ -646,7 +957,7 @@
         x = nxt
     block_out = x.reshape(rows, length, width)
     dx = cotangent.reshape(total, width)
-    big, small_gain, small_gate = [None] * LAYERS, [None] * LAYERS, [None] * LAYERS
+    big, small = [None] * LAYERS, [None] * LAYERS
     for k in reversed(range(LAYERS)):
         (w_in, w_out, w_ffn, w_down, x, proj, normed, lam, state, prior, mixed, mid,
          normed2, gu, hid) = saved[k]
@@ -663,20 +974,25 @@
             contract_rows(normed2, d_gu),
             contract_rows(hid, dz),
         )
-        small_gain[k] = jnp.stack(
-            [jnp.sum(dg_b, axis=0), jnp.sum(dg_a[:8], axis=0), jnp.sum(dg_a[8:], axis=0)]
+        small[k] = jnp.stack(
+            [
+                jnp.sum(dg_b, axis=0),
+                jnp.sum(dg_a[:8], axis=0),
+                jnp.sum(dg_a[8:], axis=0),
+                jnp.concatenate([jnp.sum(dgate[:8], axis=0), jnp.sum(dgate[8:], axis=0)]),
+            ]
         )
-        small_gate[k] = jnp.stack([jnp.sum(dgate[:8], axis=0), jnp.sum(dgate[8:], axis=0)])
-    d_gains, d_gate_params = lax.psum(
-        (jnp.stack(small_gain), jnp.stack(small_gate)), ("batch", "seq")
-    )
-    outs = []
-    for m in range(4):
-        parts = []
-        for k in range(LAYERS):
-            part = lax.psum_scatter(big[k][m], "batch", scatter_dimension=0, tiled=True)
-            parts.append(lax.psum(part, "seq").astype(F32))
-        outs.append(jnp.stack(parts))
+        if paired:
+            big[k], rows_8 = scatter(n, big[k], jnp.pad(small[k], ((0, 4), (0, 0))))
+            small[k] = rows_8[:4]
+        else:
+            parts = [lax.psum_scatter(g, "batch", scatter_dimension=0, tiled=True) for g in big[k]]
+            big[k] = [lax.psum(part, "seq").astype(F32) for part in parts]
+            small[k] = lax.psum(small[k], ("batch", "seq"))
+    totals = jnp.stack(small)
+    d_gains = totals[:, :3]
+    d_gate_params = totals[:, 3].reshape(LAYERS, 2, chan)
+    outs = [jnp.stack([big[k][m] for k in range(LAYERS)]) for m in range(4)]
     return (block_out, dx.reshape(rows, length, width), *outs, d_gains, d_gate_params)
 
 

time: 1260 us -> 505 us (0.40)
  waiting for transfers between devices: 890 us -> 0 us
  Pallas kernels: 200 us -> 426 us
  blocking collectives: 41.3 us -> 0 us
  local copies, waits for them, and re-layouts: 43.1 us -> 24.4 us
  between operations: 14.6 us -> 1.36 us
    reduce_scatter x8 -> x0, waiting for transfers between devices: 478 us -> none  [shards(): part = lax.psum_scatter(big[k][m], 'batch', scatter_dimension=0, tiled=True)]
    all_gather x8 -> x0, waiting for transfers between devices: 385 us -> none  [the longest x2 162 us: shards(): w_ffn = lax.all_gather(ffn_in[k], 'batch', axis=0, tiled=True)]
    pallas_call x0 -> x3, Pallas kernels: none -> 224 us  [the longest x2 133 us: scatter(): pl.pallas_call(functools.partial(scatter_kernel, n, mats), out_shape=[jax...]
    psum x1 -> x0, blocking collectives: 41.3 us -> none  [shards(): lax.psum((jnp.stack(small_gain), jnp.stack(small_gate)), ('batch', 'seq'))]
    psum x1 -> x0, waiting for transfers between devices: 24.8 us -> none  [shards(): parts.append(lax.psum(part, 'seq').astype(F32))]
    unnamed x102 -> x80, local copies, waits for them, and re-layouts: 32.3 us -> 18.9 us
  transfers between devices with their start and end apart: 17 -> 0, of which waited for: 15 -> 0; matrix products, arithmetic and copies ran while one was open for 5% -> 0% of each run, Pallas kernels for 12% -> 0%
where the time goes in v2:
time: 505 us; the launch traced here: 502 us
  Pallas kernels  426 us (84%)
  matrix products  42.6 us (8%)
  local copies, waits for them, and re-layouts  24.4 us (5%)
  other arithmetic  8.09 us (2%)
    pallas_call x2, Pallas kernels, scatter(): pl.pallas_call(functools.partial(scatter_kernel, n, mats), out_shape=[jax...  133 us
    pallas_call x1, Pallas kernels, gather(): pl.pallas_call(functools.partial(gather_kernel, n, layers, mats), out_sha...  90.4 us
    pallas_call x2, Pallas kernels, shards(): back_out(dx, gu, mid, state, proj[:, 3 * chan:], lam, w_out, w_ffn, w_dow...  61.3 us
    pallas_call x2, Pallas kernels, shards(): leave(F32 if k + 1 < LAYERS else BF16)  51.8 us
    dot_general x8, matrix products, contract_rows(): lax.dot_general(left, right, (((0,), (0,)), ((), ())), preferred_element_...  42.6 us
    pallas_call x2, Pallas kernels, shards(): back_in(rel, x, d_mid, proj, d_pg, lam, prior, g, cum, ends, carry, w_in,...  39.4 us
    pallas_call x2, Pallas kernels, shards(): enter(rel, x, w_in, gain_rows[k], gate_rows[k])  28.3 us
    unnamed x80, local copies, waits for them, and re-layouts  18.9 us

profile of v2, /device:TPU:0, one launch (start us, length us, event | category | flops | bytes accessed | tf_op | source)
XLA Modules:
  0.0 502.1 jit_solution(8932059500874879960)
XLA Ops:
  3.8 90.4 %shard_map.152 = (bf16[8,96,1920]{2,1,0:T(8,128)(2,1)}, bf16[8,96,768]{2,1,0:T(8,128)(2,1)}, bf16[8,96,3072]{2,1,0:T(8,128)(2,1)}, bf16[8,192,768]{2,1,0:T(8,128...) custom-call(bf16[2,96,1920]{2,1,0:T(8,128)(2,1)} %refs_0_.1, ...), custom_call_target="tpu_custom_call" | custom-call | tf_op jit(solution)/shard_map/pallas_call | solution.py:510
  94.2 14.3 %shard_map.153 = (bf16[1024,1920]{1,0:T(8,128)(2,1)}, bf16[1024,768]{1,0:T(8,128)(2,1)S(1)}, f32[3,1024,128]{2,1,0:T(8,128)S(1)}, f32[6,1024,128]{2,1,0:T(8,128)...) custom-call(s32[2,6]{1,0:T(2,128)S(1)} %broadcast_subtract_fusion.rel_ref, ...), custom_call_target="tpu_custom_call" | custom-call | tf_op jit(solution)/shard_map/pallas_call | solution.py:950
  112.6 5.4 %shard_map.154.carry_ref = f32[2,8,384]{2,1,0:T(8,128)} custom-call(f32[2,8,384]{2,1,0:T(8,128)} %copy-done.22, f32[3,384]{1,0:T(4,128)} %get-tuple-element.181.rot_ref), custom_call_target="tpu_custom_call" | custom-call | tf_op jit(solution)/shard_map/pallas_call | solution.py:951
  118.1 2.7 slice.88.proj_ref
  120.7 25.7 %shard_map.155 = (f32[6,1024,128]{2,1,0:T(8,128)}, f32[6,1024,128]{2,1,0:T(8,128)}, bf16[1024,768]{1,0:T(8,128)(2,1)S(1)}, f32[1024,768]{1,0:T(8,128)}, bf16[102...) custom-call(bf16[1024,768]{1,0:T(8,128)(2,1)S(1)} %bitcast.61, ...), custom_call_target="tpu_custom_call" | custom-call | tf_op jit(solution)/shard_map/pallas_call | solution.py:952
  148.7 14.0 %shard_map.156 = (bf16[1024,1920]{1,0:T(8,128)(2,1)}, bf16[1024,768]{1,0:T(8,128)(2,1)S(1)}, f32[3,1024,128]{2,1,0:T(8,128)S(1)}, f32[6,1024,128]{2,1,0:T(8,128)...) custom-call(s32[2,6]{1,0:T(2,128)S(1)} %broadcast_subtract_fusion.rel_ref, ...), custom_call_target="tpu_custom_call" | custom-call | tf_op jit(solution)/shard_map/pallas_call | solution.py:950
  166.9 5.3 %shard_map.157.carry_ref = f32[2,8,384]{2,1,0:T(8,128)} custom-call(f32[2,8,384]{2,1,0:T(8,128)} %copy-done.23, f32[3,384]{1,0:T(4,128)} %get-tuple-element.180.rot_ref), custom_call_target="tpu_custom_call" | custom-call | tf_op jit(solution)/shard_map/pallas_call | solution.py:951
  173.8 26.2 %shard_map.158 = (f32[6,1024,128]{2,1,0:T(8,128)}, f32[6,1024,128]{2,1,0:T(8,128)}, bf16[1024,768]{1,0:T(8,128)(2,1)S(1)}, f32[1024,768]{1,0:T(8,128)}, bf16[102...) custom-call(f32[1024,768]{1,0:T(8,128)} %get-tuple-element.93.x_ref,, ...), custom_call_target="tpu_custom_call" | custom-call | tf_op jit(solution)/shard_map/pallas_call | solution.py:952
  201.2 30.8 %shard_map.159 = (bf16[1024,768]{1,0:T(8,128)(2,1)S(1)}, bf16[1024,3072]{1,0:T(8,128)(2,1)}, f32[1024,768]{1,0:T(8,128)}, bf16[1024,768]{1,0:T(8,128)(2,1)S(1)},...) custom-call(bf16[1024,768]{1,0:T(8,128)(2,1)} %bitcast.91, ...), custom_call_target="tpu_custom_call" | custom-call | tf_op jit(solution)/shard_map/pallas_call | solution.py:964
  232.0 3.9 convolution_convert_fusion.2
  236.0 2.5 convolution_convert_fusion.6
  238.5 5.3 %shard_map.160.carry_ref = f32[2,8,384]{2,1,0:T(8,128)} custom-call(f32[2,8,384]{2,1,0:T(8,128)} %copy-done.21, f32[3,384]{1,0:T(4,128)} %get-tuple-element.180.rot_ref), custom_call_target="tpu_custom_call" | custom-call | tf_op jit(solution)/shard_map/pallas_call | solution.py:967
  247.3 19.8 %shard_map.161 = (bf16[1024,1920]{1,0:T(8,128)(2,1)}, f32[1024,768]{1,0:T(8,128)}, f32[8,768]{1,0:T(8,128)S(1)}, f32[16,384]{1,0:T(8,128)S(1)}) custom-call(s32[2,6]{1,0:T(2,128)S(1)} %broadcast_subtract_fusion.rel_ref, f32[1024,768]{1,0:T(8,128)} %get-tuple-element.93.x_ref, f32[1024,768]{1,0:T(8,128)} %get-tuple-element.108.dmid_ref, ...), custom_call_target="tpu_custom_call" | custom-call | tf_op jit(solution)/shard_map/pallas_call | solution.py:968
  267.1 30.5 %shard_map.162 = (bf16[1024,768]{1,0:T(8,128)(2,1)S(1)}, bf16[1024,3072]{1,0:T(8,128)(2,1)}, f32[1024,768]{1,0:T(8,128)}, bf16[1024,768]{1,0:T(8,128)(2,1)S(1)},...) custom-call(f32[1024,768]{1,0:T(8,128)} %get-tuple-element.115.dx_re, ...), custom_call_target="tpu_custom_call" | custom-call | tf_op jit(solution)/shard_map/pallas_call | solution.py:964
  297.6 4.0 convolution_convert_fusion.3
  304.3 5.3 %shard_map.163.carry_ref = f32[2,8,384]{2,1,0:T(8,128)} custom-call(f32[2,8,384]{2,1,0:T(8,128)} %copy-done.20, f32[3,384]{1,0:T(4,128)} %get-tuple-element.181.rot_ref), custom_call_target="tpu_custom_call" | custom-call | tf_op jit(solution)/shard_map/pallas_call | solution.py:967
  311.8 19.6 %shard_map.164 = (bf16[1024,1920]{1,0:T(8,128)(2,1)}, f32[1024,768]{1,0:T(8,128)}, f32[8,768]{1,0:T(8,128)S(1)}, f32[16,384]{1,0:T(8,128)S(1)}) custom-call(s32[2,6]{1,0:T(2,128)S(1)} %broadcast_subtract_fusion.rel_ref, bf16[1024,768]{1,0:T(8,128)(2,1)S(1)} %bitcast.62, f32[1024,768]{1,0:T(8,128)} %get-tuple-element.120.dmid_ref, ...), custom_call_target="tpu_custom_call" | custom-call | tf_op jit(solution)/shard_map/pallas_call | solution.py:968
  331.5 7.9 %convolution_convert_fusion.5 = bf16[768,1920]{1,0:T(8,128)(2,1)} fusion(bf16[1024,768]{1,0:T(8,128)(2,1)} %copy-done.24, bf16[1024,1920]{1,0:T(8,128)(2,1)} %get-tuple-element.129), kind=kOutput, calls=%fused_computation.5 | convolution fusion | flops 3021373440 | bytes 8454144 | tf_op jit(solution)/shard_map/dot_general | solution.py:909
  339.4 4.9 convolution_convert_fusion.4
  344.3 9.7 %convolution_convert_fusion.1 = bf16[768,3072]{1,0:T(8,128)(2,1)} fusion(bf16[1024,768]{1,0:T(8,128)(2,1)S(1)} %copy-done.26, bf16[1024,3072]{1,0:T(8,128)(2,1)} %get-tuple-element.133), kind=kOutput, calls=%fused_computation.1 | convolution fusion | flops 4834197504 | bytes 12582912 | tf_op jit(solution)/shard_map/dot_general | solution.py:909
  354.0 67.0 %shard_map.165 = (f32[96,1920]{1,0:T(8,128)S(1)}, f32[96,768]{1,0:T(8,128)S(1)}, f32[96,3072]{1,0:T(8,128)}, f32[192,768]{1,0:T(8,128)S(1)}, f32[8,768]{1,0:T(8,128)S(1)}) custom-call(bf16[8,96,1920]{2,1,0:T(8,128)(2,1)} %bitcast.88, bf16[8,96,768]{2,1,0:T(8,128)(2,1)} %bitcast.93, bf16[8,96,3072]{2,1,0:T(8,128)(2,1)} %bitcast.85, ...), custom_call_target="tpu_custom_call" | custom-call | tf_op jit(solution)/shard_map/pallas_call | solution.py:677
  421.1 7.2 %convolution_convert_fusion = bf16[768,3072]{1,0:T(8,128)(2,1)} fusion(bf16[1024,768]{1,0:T(8,128)(2,1)S(1)} %copy-done.28, bf16[1024,3072]{1,0:T(8,128)(2,1)S(1)} %bitcast.97), kind=kOutput, calls=%fused_computation | convolution fusion | flops 4834197504 | bytes 12582912 | tf_op jit(solution)/shard_map/dot_general | solution.py:909
  428.3 66.1 %shard_map.166 = (f32[96,1920]{1,0:T(8,128)S(1)}, f32[96,768]{1,0:T(8,128)S(1)}, f32[96,3072]{1,0:T(8,128)}, f32[192,768]{1,0:T(8,128)S(1)}, f32[8,768]{1,0:T(8,128)S(1)}) custom-call(bf16[8,96,1920]{2,1,0:T(8,128)(2,1)} %bitcast.87, bf16[8,96,768]{2,1,0:T(8,128)(2,1)} %bitcast.92, bf16[8,96,3072]{2,1,0:T(8,128)(2,1)} %bitcast.86, ...), custom_call_target="tpu_custom_call" | custom-call | tf_op jit(solution)/shard_map/pallas_call | solution.py:677
  498.8 3.0 pad_maximum_fusion
  (115 shorter events, 29.3 us)
Async XLA Ops:
  112.6 8.1 %copy-start = (bf16[2,512,768]{2,1,0:T(8,128)(2,1)S(1)}, bf16[2,512,768]{2,1,0:T(8,128)(2,1)}, u32[]{:S(2)}) copy-start(bf16[2,512,768]{2,1,0:T(8,128)(2,1)} %param.9) | copy-start | bytes 4718596
  112.6 8.1 %copy-start.6 = (bf16[8,96,768]{2,1,0:T(8,128)(2,1)S(1)}, bf16[8,96,768]{2,1,0:T(8,128)(2,1)}, u32[]{:S(2)}) copy-start(bf16[8,96,768]{2,1,0:T(8,128)(2,1)} %get-tuple-element.90) | copy-start | bytes 3538948
  118.0 2.7 copy-start.18
  166.9 6.9 %copy-start.8 = (bf16[8,96,768]{2,1,0:T(8,128)(2,1)S(1)}, bf16[8,96,768]{2,1,0:T(8,128)(2,1)}, u32[]{:S(2)}) copy-start(bf16[8,96,768]{2,1,0:T(8,128)(2,1)} %get-tuple-element.100) | copy-start | bytes 3538948
  172.3 1.5 copy-start.19
  173.8 26.2 %copy-start.1 = (bf16[1024,768]{1,0:T(8,128)(2,1)}, bf16[1024,768]{1,0:T(8,128)(2,1)S(1)}, u32[]{:S(2)}) copy-start(bf16[1024,768]{1,0:T(8,128)(2,1)S(1)} %slice.92.proj_ref) | copy-start | bytes 4718596
  201.2 30.8 %copy-start.36 = (bf16[1024,1536]{1,0:T(8,128)(2,1)S(1)}, bf16[1024,1536]{1,0:T(8,128)(2,1)}, u32[]{:S(2)}) copy-start(bf16[1024,1536]{1,0:T(8,128)(2,1)} %get-tuple-element.146) | copy-start | bytes 9437188
  232.0 4.0 copy-start.11
  232.0 4.0 copy-start.21
  236.0 7.8 %copy-start.5 = (f32[3,1024,128]{2,1,0:T(8,128)S(1)}, f32[3,1024,128]{2,1,0:T(8,128)}, u32[]{:S(2)}) copy-start(f32[3,1024,128]{2,1,0:T(8,128)} %copy-done.4) | copy-start | bytes 4718596
  247.3 19.8 %copy-start.7 = (bf16[8,96,768]{2,1,0:T(8,128)(2,1)S(1)}, bf16[8,96,768]{2,1,0:T(8,128)(2,1)}, u32[]{:S(2)}) copy-start(bf16[8,96,768]{2,1,0:T(8,128)(2,1)} %get-tuple-element.90) | copy-start | bytes 3538948
  267.1 30.5 %copy-start.35 = (bf16[1024,1536]{1,0:T(8,128)(2,1)S(1)}, bf16[1024,1536]{1,0:T(8,128)(2,1)}, u32[]{:S(2)}) copy-start(bf16[1024,1536]{1,0:T(8,128)(2,1)} %get-tuple-element.134) | copy-start | bytes 9437188
  297.6 4.1 copy-start.9
  297.6 4.1 copy-start.20
  297.6 4.0 copy-start.32
  301.7 7.9 %copy-start.3 = (f32[3,1024,128]{2,1,0:T(8,128)S(1)}, f32[3,1024,128]{2,1,0:T(8,128)}, u32[]{:S(2)}) copy-start(f32[3,1024,128]{2,1,0:T(8,128)} %copy-done.2) | copy-start | bytes 4718596
  309.6 1.4 copy-start.10
  331.5 7.9 %copy-start.30 = (bf16[1024,768]{1,0:T(8,128)(2,1)S(1)}, bf16[1024,768]{1,0:T(8,128)(2,1)}, u32[]{:S(2)}) copy-start(bf16[1024,768]{1,0:T(8,128)(2,1)} %copy-done.29) | copy-start | bytes 4718596
  331.5 7.9 %copy-start.34 = (bf16[1024,1920]{1,0:T(8,128)(2,1)S(1)}, bf16[1024,1920]{1,0:T(8,128)(2,1)}, u32[]{:S(2)}) copy-start(bf16[1024,1920]{1,0:T(8,128)(2,1)} %get-tuple-element.141) | copy-start | bytes 11796484
  339.4 4.9 copy-start.26
  339.4 81.6 %slice-start = ((s8[6291456]{0:T(1024)(128)(4,1)}), s8[4194304]{0:T(1024)(128)(4,1)S(1)}, s32[]{:S(2)}) async-start(s8[6291456]{0:T(1024)(128)(4,1)} %bitcast.96), calls=%async_computation | async-start | bytes 8388608
  344.3 76.8 %slice-start.1 = ((s8[6291456]{0:T(1024)(128)(4,1)}), s8[2097152]{0:T(1024)(128)(4,1)S(1)}, s32[]{:S(2)}) async-start(s8[6291456]{0:T(1024)(128)(4,1)} %bitcast.96), calls=%async_computation.1 | async-start | bytes 4194304
  354.0 67.0 %copy-start.28 = (bf16[1024,768]{1,0:T(8,128)(2,1)S(1)}, bf16[1024,768]{1,0:T(8,128)(2,1)}, u32[]{:S(2)}) copy-start(bf16[1024,768]{1,0:T(8,128)(2,1)} %copy-done.27) | copy-start | bytes 4718596
  495.6 3.2 copy-start.33
  (15 other events, 16.1 us)

commit v3 on v2

--- a/solution.py
+++ b/solution.py
@@ -12,6 +12,7 @@
 F32 = jnp.float32
 BF16 = jnp.bfloat16
 LANES = 128
+CHUNK = 768
 MESH = pl.DeviceIdType.MESH
 
 
@@ -532,23 +533,51 @@
     lax.fori_loop(0, rows // 16, block, 0)
 
 
-def scatter_kernel(n, mats, *refs):
-    grads, small = refs[:mats], refs[mats]
-    outs, small_out = refs[mats + 1 : 2 * mats + 1], refs[2 * mats + 1]
-    rest = refs[2 * mats + 2 :]
-    core_buf, y_out, y_buf, ring_out, ring_buf = (rest[i * mats : (i + 1) * mats] for i in range(5))
-    fin, fin_buf, half, half_buf = (rest[(5 + i) * mats : (6 + i) * mats] for i in range(4))
-    small_buf, core_send, core_recv, y_send, y_recv, ring_send, ring_recv, end_send, end_recv, small_send, small_recv = rest[9 * mats :]
+def grads_kernel(n, plan, *refs):
+    jobs = len(plan)
+    lefts, rights, small = refs[:jobs], refs[jobs : 2 * jobs], refs[2 * jobs]
+    outs_count = 1 + max(p[0] for p in plan)
+    outs, small_out = refs[2 * jobs + 1 : 2 * jobs + 1 + outs_count], refs[2 * jobs + 1 + outs_count]
+    rest = refs[2 * jobs + 2 + outs_count :]
+    grads, core_buf, y_buf, ring_buf, fin_buf = (rest[i * jobs : (i + 1) * jobs] for i in range(5))
+    (left_big, left_small, right_buf, small_buf, left_sem, right_sem, core_send, core_recv, y_send, y_recv,
+     ring_send, ring_recv, end_send, end_recv, small_send, small_recv) = rest[5 * jobs :]
     ring = Ring(n)
     far, near = n // 2, n - 1 - n // 2
     core_dev, y_dev = {"seq": ring.core_peer}, {"seq": ring.y_peer}
+    y, core = ring.y, ring.core
     rounds = [core_dev, y_dev]
     d = 1
     while d < n:
         rounds.append({"batch": ring.batch + d * (1 - 2 * ((ring.batch // d) % 2))})
         d *= 2
+    us = [g.shape[0] // n // 6 for g in grads]
+    split = [p[2] for p in plan]
+    own_rows = [(2 if s else 3) * u for s, u in zip(split, us)]
+
+    def left_copy(j):
+        buf = (left_big, left_small)[j % 2]
+        return pltpu.make_async_copy(lefts[j], buf.at[:, 0 : plan[j][3]], left_sem.at[j % 2])
+
+    chunks = []
+    for j, (_, _, _, rows, cols) in enumerate(plan):
+        first = 0
+        while first < cols:
+            size = min(CHUNK, cols - first)
+            chunks.append((j, first, size, first + size == cols))
+            first += size
+
+    def right_copy(i):
+        j, first, size, _ = chunks[i]
+        return pltpu.make_async_copy(
+            rights[j].at[:, first : first + size], right_buf.at[i % 2, :, 0:size], right_sem.at[i % 2]
+        )
+
+    left_copy(0).start()
+    right_copy(0).start()
+    right_copy(1).start()
+    left_copy(1).start()
     meet([{"batch": ring.ahead(1)}, {"batch": ring.ahead(-1)}] + rounds)
-    us = [g.shape[1] // 6 for g in grads]
 
     order = []
     for h in range(far):
@@ -556,149 +585,219 @@
         if h < near:
             order.append((-1, h, near - h))
     order.append((0, 0, 0))
-
-    def core_copy(m, slot, piece):
-        u = us[m]
-        return remote(
-            grads[m].at[piece, pl.ds(pl.multiple_of((1 - ring.core) * (3 * u), 16), 3 * u)],
-            core_buf[m].at[slot], core_send.at[m], core_recv.at[m, slot], core_dev,
-        )
-
-    def y_copy(m, slot):
-        return remote(y_out[m].at[slot], y_buf[m].at[slot], y_send.at[m], y_recv.at[m, slot], y_dev)
-
-    def ring_copy(m, slot, way):
-        return remote(ring_out[m].at[slot], ring_buf[m].at[slot], ring_send.at[m], ring_recv.at[m, slot],
-                      {"batch": ring.ahead(way)})
-
-    for slot, (way, h, dist) in enumerate(order):
-        for m in range(mats):
-            core_copy(m, slot, ring.ahead(-way * dist)).start()
-    small_buf[0] = small[...]
+    last = len(order)
+
+    def rows_at(ref, first, rows):
+        return ref.at[pl.ds(pl.multiple_of(first, 16), rows)]
+
+    def core_copy(j, slot, piece):
+        u = us[j]
+        return remote(rows_at(grads[j], piece * (6 * u) + (1 - core) * (3 * u), 3 * u),
+                      core_buf[j].at[slot], core_send.at[j], core_recv.at[j, slot], core_dev)
+
+    def y_copy(j, slot, piece):
+        u = us[j]
+        src = rows_at(grads[j], piece * (6 * u) + core * (3 * u) + 2 * (1 - y) * u, u)
+        return remote(src, y_buf[j].at[slot], y_send.at[j], y_recv.at[j, slot], y_dev)
+
+    def mine(j, piece):
+        u = us[j]
+        return piece * (6 * u) + core * (3 * u) + (y * u if split[j] else 0)
+
+    def ring_copy(j, slot, way, piece):
+        return remote(rows_at(grads[j], mine(j, piece), own_rows[j]), ring_buf[j].at[slot], ring_send.at[j],
+                      ring_recv.at[j, slot], {"batch": ring.ahead(way)})
 
     def small_round(r):
         return remote(small_buf.at[2 * r], small_buf.at[2 * r + 1], small_send.at[r], small_recv.at[r], rounds[r])
 
+    small_buf[0] = small[...]
     small_round(0).start()
 
-    def cross(slot):
+    def small_step(r):
+        small_round(r).wait_recv()
+        total = small_buf[2 * r] + small_buf[2 * r + 1]
+        if r + 1 < len(rounds):
+            small_buf[2 * r + 2] = total
+            small_round(r + 1).start()
+        else:
+            small_out[...] = total
+
+    def begin(j):
+        for slot, (way, h, dist) in enumerate(order):
+            core_copy(j, slot, ring.ahead(-way * dist)).start()
+
+    def cross(j, slot):
         way, h, dist = order[slot]
         piece = ring.ahead(way * dist)
-        for m in range(mats):
-            u = us[m]
-            core_copy(m, slot, piece).wait_recv()
-            give = 2 * (1 - ring.y) * u
-            add_rows(y_out[m].at[slot], 0, [(grads[m].at[piece], ring.core * (3 * u) + give),
-                                            (core_buf[m].at[slot], give)], u)
-            y_copy(m, slot).start()
-
-    def hop(slot):
+        u = us[j]
+        core_copy(j, slot, piece).wait_recv()
+        if not split[j]:
+            return
+        give = 2 * (1 - y) * u
+        at = piece * (6 * u) + core * (3 * u) + give
+        add_rows(grads[j], at, [(grads[j], at), (core_buf[j].at[slot], give)], u)
+        y_copy(j, slot, piece).start()
+
+    def hop(j, slot):
         way, h, dist = order[slot]
         piece = ring.ahead(way * dist)
-        for m in range(mats):
-            u = us[m]
-            y_copy(m, slot).wait_recv()
-            extra = []
-            if way == 0:
-                prior = [i for i, o in enumerate(order) if o[2] == 1]
-            elif h:
-                prior = [i for i, o in enumerate(order) if o[0] == way and o[1] == h - 1]
-            else:
-                prior = []
-            for i in prior:
-                ring_copy(m, i, order[i][0]).wait_recv()
-            target = fin[m] if way == 0 else ring_out[m].at[slot]
-            own = ring.y * u
-            rest_ = (1 - ring.y) * u
-            base = [(grads[m].at[piece], ring.core * (3 * u) + ring.y * u), (core_buf[m].at[slot], ring.y * u)]
-            more = [(ring_buf[m].at[i], 0) for i in prior]
-            shift = lambda parts, by: [(r, f + by) for r, f in parts]
-            add_rows(target, own, shift(base + more, own) + [(y_buf[m].at[slot], 0)], u)
-            add_rows(target, rest_, shift(base + more, rest_), u)
-            if way:
-                ring_copy(m, slot, way).start()
-
-    def end_copy(m, kind):
-        src, dst, device = ((fin[m], fin_buf[m], y_dev), (half[m], half_buf[m], core_dev))[kind]
-        return remote(src, dst, end_send.at[m, kind], end_recv.at[m, kind], device)
-
-    last = len(order)
+        u = us[j]
+        if split[j]:
+            y_copy(j, slot, piece).wait_recv()
+        if way == 0:
+            prior = [i for i, o in enumerate(order) if o[2] == 1]
+        elif h:
+            prior = [i for i, o in enumerate(order) if o[0] == way and o[1] == h - 1]
+        else:
+            prior = []
+        for i in prior:
+            ring_copy(j, i, order[i][0], piece).wait_recv()
+        at = mine(j, piece)
+        base = [(grads[j], at), (core_buf[j].at[slot], y * u if split[j] else 0)]
+        base += [(ring_buf[j].at[i], 0) for i in prior]
+        if split[j]:
+            for by, more in ((y * u, [(y_buf[j].at[slot], 0)]), ((1 - y) * u, [])):
+                add_rows(grads[j], at + by, [(r, f + by) for r, f in base] + more, u)
+        else:
+            add_rows(grads[j], at, base, 3 * u)
+        if way:
+            ring_copy(j, slot, way, piece).start()
+
+    def fin_copy(j):
+        return remote(rows_at(grads[j], mine(j, ring.batch), own_rows[j]), fin_buf[j], end_send.at[j, 0],
+                      end_recv.at[j, 0], y_dev)
+
+    def half_copy(j):
+        half = outs[plan[j][0]].at[plan[j][1], pl.ds(pl.multiple_of(core * (3 * us[j]), 16), 3 * us[j])]
+        return remote(half, half, end_send.at[j, 1], end_recv.at[j, 1], core_dev)
+
+    def finish(j):
+        u = us[j]
+        fin_copy(j).wait_recv()
+        out = outs[plan[j][0]].at[plan[j][1]]
+        at, to = mine(j, ring.batch), core * (3 * u)
+        if split[j]:
+            add_rows(out, to + 2 * y * u, [(grads[j], at + y * u)], u)
+            add_rows(out, to + 2 * (1 - y) * u, [(fin_buf[j], (1 - y) * u)], u)
+            add_rows(out, to + u, [(grads[j], at + (1 - y) * u), (fin_buf[j], y * u)], u)
+        else:
+            add_rows(out, to, [(grads[j], at), (fin_buf[j], 0)], 3 * u)
+        half_copy(j).start()
+
+    steps = far + 4
+
+    def advance(j, t):
+        now = [i for i, o in enumerate(order) if o[0] and o[1] == t]
+        before = [i for i, o in enumerate(order) if o[0] and o[1] == t - 1]
+        for slot in before:
+            hop(j, slot)
+        for slot in now:
+            cross(j, slot)
+        if t == far - 1:
+            cross(j, last - 1)
+        if t == far + 1:
+            hop(j, last - 1)
+            fin_copy(j).start()
+        if t == far + 2:
+            finish(j)
+        if t == far + 3:
+            half_copy(j).wait_recv()
+
+    stage = {}
+
+    def advance_all(turn):
+        for j in list(stage):
+            if j % 2 == turn:
+                advance(j, stage[j])
+                stage[j] += 1
+                if stage[j] == steps:
+                    del stage[j]
+
     small_at = 0
-    for t in range(last + 1):
-        if t < last:
-            cross(t)
-        if t >= 1:
-            hop(t - 1)
-        if t >= 1 and small_at < len(rounds):
-            small_round(small_at).wait_recv()
-            total = small_buf[2 * small_at] + small_buf[2 * small_at + 1]
+    for i, (j, first, size, done) in enumerate(chunks):
+        if first == 0:
+            left_copy(j).wait()
+        right_copy(i).wait()
+        left = (left_big, left_small)[j % 2]
+
+        def multiply(b, _, i=i, j=j, first=first, size=size, left=left):
+            at = pl.multiple_of(b * 256, 256)
+            part = lax.dot_general(
+                left[:, pl.ds(at, 256)], right_buf[i % 2, :, 0:size], (((0,), (0,)), ((), ())),
+                preferred_element_type=F32,
+            )
+            grads[j][pl.ds(at, 256), first : first + size] = part.astype(BF16)
+            return 0
+
+        lax.fori_loop(0, plan[j][3] // 256, multiply, 0)
+        if i + 2 < len(chunks):
+            right_copy(i + 2).start()
+        if done and j + 2 < jobs:
+            left_copy(j + 2).start()
+        advance_all(i % 2)
+        if done:
+            begin(j)
+            stage[j] = 0
+        if small_at < len(rounds):
+            small_step(small_at)
             small_at += 1
-            if small_at < len(rounds):
-                small_buf[2 * small_at] = total
-                small_round(small_at).start()
-            else:
-                small_out[...] = total
-    for m in range(mats):
-        end_copy(m, 0).start()
-    for m in range(mats):
-        u = us[m]
-        y = ring.y
-        end_copy(m, 0).wait_recv()
-        add_rows(half[m], 2 * y * u, [(fin[m], y * u)], u)
-        add_rows(half[m], 2 * (1 - y) * u, [(fin_buf[m], (1 - y) * u)], u)
-        add_rows(half[m], u, [(fin[m], (1 - y) * u), (fin_buf[m], y * u)], u)
-        end_copy(m, 1).start()
-        add_rows(outs[m], ring.core * (3 * u), [(half[m], 0)], 3 * u)
-    for m in range(mats):
-        u = us[m]
-        end_copy(m, 1).wait_recv()
-        add_rows(outs[m], (1 - ring.core) * (3 * u), [(half_buf[m], 0)], 3 * u)
-    for m in range(mats):
-        end_copy(m, 0).wait_send()
-        end_copy(m, 1).wait_send()
-        remote(core_buf[m], core_buf[m], core_send.at[m], core_recv.at[m, 0], core_dev).wait_send()
-        remote(y_out[m], y_buf[m], y_send.at[m], y_recv.at[m, 0], y_dev).wait_send()
-        remote(ring_out[m], ring_buf[m], ring_send.at[m], ring_recv.at[m, 0], core_dev).wait_send()
+    i = 0
+    while stage:
+        advance_all(i % 2)
+        i += 1
+    while small_at < len(rounds):
+        small_step(small_at)
+        small_at += 1
+    for j in range(jobs):
+        u = us[j]
+        fin_copy(j).wait_send()
+        half_copy(j).wait_send()
+        remote(core_buf[j], core_buf[j], core_send.at[j], core_recv.at[j, 0], core_dev).wait_send()
+        if split[j]:
+            remote(y_buf[j], y_buf[j], y_send.at[j], y_recv.at[j, 0], y_dev).wait_send()
+        remote(ring_buf[j], ring_buf[j], ring_send.at[j], ring_recv.at[j, 0], core_dev).wait_send()
     for r in range(len(rounds)):
         small_round(r).wait_send()
 
 
-def scatter(n, grads, small):
-    mats = len(grads)
-    grads = [g.reshape(n, g.shape[0] // n, g.shape[1]) for g in grads]
-    us = [(g.shape[1] // 6, g.shape[2]) for g in grads]
+def grads_and_scatter(n, plan, lefts, rights, small):
+    jobs = len(plan)
+    plan = [p + (a.shape[1], b.shape[1]) for p, a, b in zip(plan, lefts, rights)]
+    tokens = lefts[0].shape[0]
+    layers = 1 + max(p[1] for p in plan)
     dma = pltpu.SemaphoreType.DMA
+    rounds = 2 + (n - 1).bit_length()
+    sizes = [(p[3] // n // 6, p[4], p[2]) for p in plan]
+    outs = {p[0]: jax.ShapeDtypeStruct((layers, p[3] // n, p[4]), BF16) for p in plan}
     vm = pl.BlockSpec(memory_space=pltpu.VMEM)
-    rounds = 2 + (n - 1).bit_length()
+    any_ = pl.BlockSpec(memory_space=pl.ANY)
 
     def bufs(f):
-        return [pltpu.VMEM(f(u, w), BF16) for u, w in us]
-
-    outs = pl.pallas_call(
-        functools.partial(scatter_kernel, n, mats),
-        out_shape=[jax.ShapeDtypeStruct(g.shape[1:], F32) for g in grads]
-        + [jax.ShapeDtypeStruct(small.shape, F32)],
-        in_specs=[vm] * (mats + 1),
-        out_specs=[vm] * (mats + 1),
-        scratch_shapes=bufs(lambda u, w: (n, 3 * u, w))
-        + bufs(lambda u, w: (n, u, w))
-        + bufs(lambda u, w: (n, u, w))
-        + bufs(lambda u, w: (n - 1, 2 * u, w))
-        + bufs(lambda u, w: (n - 1, 2 * u, w))
-        + bufs(lambda u, w: (2 * u, w))
-        + bufs(lambda u, w: (2 * u, w))
-        + bufs(lambda u, w: (3 * u, w))
-        + bufs(lambda u, w: (3 * u, w))
+        return [pltpu.VMEM(f(u, w, s), BF16) for u, w, s in sizes]
+
+    return pl.pallas_call(
+        functools.partial(grads_kernel, n, plan),
+        out_shape=[outs[m] for m in sorted(outs)] + [jax.ShapeDtypeStruct(small.shape, F32)],
+        in_specs=[any_] * (2 * jobs) + [vm],
+        out_specs=[vm] * (len(outs) + 1),
+        scratch_shapes=bufs(lambda u, w, s: (6 * u * n, w))
+        + bufs(lambda u, w, s: (n, 3 * u, w))
+        + bufs(lambda u, w, s: (n if s else 1, u, w))
+        + bufs(lambda u, w, s: (n - 1, 2 * u if s else 3 * u, w))
+        + bufs(lambda u, w, s: (2 * u if s else 3 * u, w))
         + [
+            pltpu.VMEM((tokens, max(p[3] for p in plan[0::2])), BF16),
+            pltpu.VMEM((tokens, max(p[3] for p in plan[1::2])), BF16),
+            pltpu.VMEM((2, tokens, CHUNK), BF16),
             pltpu.VMEM((2 * rounds,) + small.shape, F32),
-            dma((mats,)), dma((mats, n)), dma((mats,)), dma((mats, n)), dma((mats,)), dma((mats, n)),
-            dma((mats, 2)), dma((mats, 2)), dma((rounds,)), dma((rounds,)),
+            dma((2,)), dma((2,)), dma((jobs,)), dma((jobs, n)), dma((jobs,)), dma((jobs, n)), dma((jobs,)),
+            dma((jobs, n)), dma((jobs, 2)), dma((jobs, 2)), dma((rounds,)), dma((rounds,)),
         ],
         compiler_params=pltpu.CompilerParams(
-            collective_id=4, has_side_effects=True, vmem_limit_bytes=52 * 1024 * 1024
+            collective_id=4, has_side_effects=True, vmem_limit_bytes=63 * 1024 * 1024
         ),
-    )(*grads, small)
-    return outs[:-1], outs[-1]
+    )(*lefts, *rights, small)
 
 
 def vmem(bytes_):
@@ -957,7 +1056,7 @@
         x = nxt
     block_out = x.reshape(rows, length, width)
     dx = cotangent.reshape(total, width)
-    big, small = [None] * LAYERS, [None] * LAYERS
+    pairs, small = [None] * LAYERS, [None] * LAYERS
     for k in reversed(range(LAYERS)):
         (w_in, w_out, w_ffn, w_down, x, proj, normed, lam, state, prior, mixed, mid,
          normed2, gu, hid) = saved[k]
@@ -968,12 +1067,7 @@
         d_proj, dx, dg_b, dgate = back_in(
             rel, x, d_mid, proj, d_pg, lam, prior, g, cum, ends, carry, w_in, gain_rows[k], gate_rows[k]
         )
-        big[k] = (
-            contract_rows(normed, d_proj),
-            contract_rows(mixed, dy),
-            contract_rows(normed2, d_gu),
-            contract_rows(hid, dz),
-        )
+        pairs[k] = ((normed, d_proj), (mixed, dy), (normed2, d_gu), (hid, dz))
         small[k] = jnp.stack(
             [
                 jnp.sum(dg_b, axis=0),
@@ -982,17 +1076,29 @@
                 jnp.concatenate([jnp.sum(dgate[:8], axis=0), jnp.sum(dgate[8:], axis=0)]),
             ]
         )
-        if paired:
-            big[k], rows_8 = scatter(n, big[k], jnp.pad(small[k], ((0, 4), (0, 0))))
-            small[k] = rows_8[:4]
-        else:
-            parts = [lax.psum_scatter(g, "batch", scatter_dimension=0, tiled=True) for g in big[k]]
-            big[k] = [lax.psum(part, "seq").astype(F32) for part in parts]
-            small[k] = lax.psum(small[k], ("batch", "seq"))
-    totals = jnp.stack(small)
+    if paired:
+        plan = []
+        for k, mats in ((LAYERS - 1, (1, 2, 3, 0)),) + tuple(
+            (k, (3, 2, 0, 1)) for k in reversed(range(LAYERS - 1))
+        ):
+            plan += [(m, k, m != 0) for m in mats]
+        *outs, totals = grads_and_scatter(
+            n, plan, [pairs[k][m][0] for m, k, _ in plan], [pairs[k][m][1] for m, k, _ in plan],
+            jnp.concatenate(small),
+        )
+        totals = totals.reshape(LAYERS, 4, width)
+    else:
+        outs = []
+        for m in range(4):
+            parts = [
+                lax.psum_scatter(contract_rows(*pairs[k][m]), "batch", scatter_dimension=0, tiled=True)
+                for k in range(LAYERS)
+            ]
+            outs.append(jnp.stack([lax.psum(part, "seq") for part in parts]))
+        totals = lax.psum(jnp.stack(small), ("batch", "seq"))
+    outs = [o.astype(F32) for o in outs]
     d_gains = totals[:, :3]
     d_gate_params = totals[:, 3].reshape(LAYERS, 2, chan)
-    outs = [jnp.stack([big[k][m] for k in range(LAYERS)]) for m in range(4)]
     return (block_out, dx.reshape(rows, length, width), *outs, d_gains, d_gate_params)
 
 

time: 505 us -> 458 us (0.907)
  matrix products: 42.6 us -> 0 us
  Pallas kernels: 426 us -> 409 us
  local copies, waits for them, and re-layouts: 24.4 us -> 34.9 us
    dot_general x8 -> x0, matrix products: 42.6 us -> none  [contract_rows(): lax.dot_general(left, right, (((0,), (0,)), ((), ())), preferred_element_...]
    pallas_call x2 -> x1, Pallas kernels: 133 us -> 117 us  [grads_and_scatter(): pl.pallas_call(functools.partial(grads_kernel, n, plan), out_shape=[outs[...]
    unnamed x80 -> x76, local copies, waits for them, and re-layouts: 18.9 us -> 28 us
    convert_element_type x0 -> x4, other arithmetic: none -> 6.98 us  [shards(): outs = [o.astype(F32) for o in outs]]
    another operation x7 -> x0, other arithmetic: 6.2 us -> none  [the longest x4 6.15 us: shards(): outs = [jnp.stack([big[k][m] for k in range(LAYERS)]) for m in range(4)]]
where the time goes in v3:
time: 458 us; the launch traced here: 454 us
  Pallas kernels  409 us (89%)
  local copies, waits for them, and re-layouts  34.9 us (8%)
  other arithmetic  8.83 us (2%)
    pallas_call x1, Pallas kernels, grads_and_scatter(): pl.pallas_call(functools.partial(grads_kernel, n, plan), out_shape=[outs[...  117 us
    pallas_call x1, Pallas kernels, gather(): pl.pallas_call(functools.partial(gather_kernel, n, layers, mats), out_sha...  90.4 us
    pallas_call x2, Pallas kernels, shards(): back_out(dx, gu, mid, state, proj[:, 3 * chan:], lam, w_out, w_ffn, w_dow...  60.6 us
    pallas_call x2, Pallas kernels, shards(): leave(F32 if k + 1 < LAYERS else BF16)  51.8 us
    pallas_call x2, Pallas kernels, shards(): back_in(rel, x, d_mid, proj, d_pg, lam, prior, g, cum, ends, carry, w_in,...  39.6 us
    pallas_call x2, Pallas kernels, shards(): enter(rel, x, w_in, gain_rows[k], gate_rows[k])  28.2 us
    unnamed x76, local copies, waits for them, and re-layouts  28 us
    pallas_call x2, Pallas kernels, shards(): carry = carry_f(tot, gate_rows[k, 5:8])  10.7 us

profile of v3, /device:TPU:0, one launch (start us, length us, event | category | flops | bytes accessed | tf_op | source)
XLA Modules:
  0.0 454.0 jit_solution(153670756511273381)
XLA Ops:
  3.8 90.4 %shard_map.152 = (bf16[8,96,1920]{2,1,0:T(8,128)(2,1)}, bf16[8,96,768]{2,1,0:T(8,128)(2,1)}, bf16[8,96,3072]{2,1,0:T(8,128)(2,1)}, bf16[8,192,768]{2,1,0:T(8,128...) custom-call(bf16[2,96,1920]{2,1,0:T(8,128)(2,1)} %refs_0_.1, ...), custom_call_target="tpu_custom_call" | custom-call | tf_op jit(solution)/shard_map/pallas_call | solution.py:511
  94.2 14.2 %shard_map.153 = (bf16[1024,1920]{1,0:T(8,128)(2,1)}, bf16[1024,768]{1,0:T(8,128)(2,1)S(1)}, f32[3,1024,128]{2,1,0:T(8,128)S(1)}, f32[6,1024,128]{2,1,0:T(8,128)...) custom-call(s32[2,6]{1,0:T(2,128)S(1)} %broadcast_subtract_fusion.rel_ref, ...), custom_call_target="tpu_custom_call" | custom-call | tf_op jit(solution)/shard_map/pallas_call | solution.py:1049
  108.4 1.2 copy-done.2
  112.5 5.4 %shard_map.154.carry_ref = f32[2,8,384]{2,1,0:T(8,128)} custom-call(f32[2,8,384]{2,1,0:T(8,128)} %copy-done.33, f32[3,384]{1,0:T(4,128)} %get-tuple-element.163.rot_ref), custom_call_target="tpu_custom_call" | custom-call | tf_op jit(solution)/shard_map/pallas_call | solution.py:1050
  118.0 2.7 slice.82.proj_ref
  120.6 25.6 %shard_map.155 = (f32[6,1024,128]{2,1,0:T(8,128)}, f32[6,1024,128]{2,1,0:T(8,128)}, bf16[1024,768]{1,0:T(8,128)(2,1)S(1)}, f32[1024,768]{1,0:T(8,128)}, bf16[102...) custom-call(bf16[1024,768]{1,0:T(8,128)(2,1)S(1)} %bitcast.26, ...), custom_call_target="tpu_custom_call" | custom-call | tf_op jit(solution)/shard_map/pallas_call | solution.py:1051
  147.4 1.2 copy-done.12
  148.6 14.0 %shard_map.156 = (bf16[1024,1920]{1,0:T(8,128)(2,1)}, bf16[1024,768]{1,0:T(8,128)(2,1)S(1)}, f32[3,1024,128]{2,1,0:T(8,128)S(1)}, f32[6,1024,128]{2,1,0:T(8,128)...) custom-call(s32[2,6]{1,0:T(2,128)S(1)} %broadcast_subtract_fusion.rel_ref, ...), custom_call_target="tpu_custom_call" | custom-call | tf_op jit(solution)/shard_map/pallas_call | solution.py:1049
  166.7 5.3 %shard_map.157.carry_ref = f32[2,8,384]{2,1,0:T(8,128)} custom-call(f32[2,8,384]{2,1,0:T(8,128)} %copy-done.34, f32[3,384]{1,0:T(4,128)} %get-tuple-element.162.rot_ref), custom_call_target="tpu_custom_call" | custom-call | tf_op jit(solution)/shard_map/pallas_call | solution.py:1050
  172.1 1.5 slice.86.proj_ref
  173.6 26.2 %shard_map.158 = (f32[6,1024,128]{2,1,0:T(8,128)}, f32[6,1024,128]{2,1,0:T(8,128)}, bf16[1024,768]{1,0:T(8,128)(2,1)S(1)}, f32[1024,768]{1,0:T(8,128)}, bf16[102...) custom-call(f32[1024,768]{1,0:T(8,128)} %get-tuple-element.88.x_ref,, ...), custom_call_target="tpu_custom_call" | custom-call | tf_op jit(solution)/shard_map/pallas_call | solution.py:1051
  202.2 30.2 %shard_map.159 = (bf16[1024,768]{1,0:T(8,128)(2,1)S(1)}, bf16[1024,3072]{1,0:T(8,128)(2,1)}, f32[1024,768]{1,0:T(8,128)}, bf16[1024,768]{1,0:T(8,128)(2,1)S(1)},...) custom-call(bf16[1024,768]{1,0:T(8,128)(2,1)} %bitcast.44, ...), custom_call_target="tpu_custom_call" | custom-call | tf_op jit(solution)/shard_map/pallas_call | solution.py:1063
  236.4 5.2 %shard_map.160.carry_ref = f32[2,8,384]{2,1,0:T(8,128)} custom-call(f32[2,8,384]{2,1,0:T(8,128)} %copy-done.32, f32[3,384]{1,0:T(4,128)} %get-tuple-element.162.rot_ref), custom_call_target="tpu_custom_call" | custom-call | tf_op jit(solution)/shard_map/pallas_call | solution.py:1066
  241.7 1.4 copy-done.23
  243.1 1.4 copy-done.24
  245.3 19.7 %shard_map.161 = (bf16[1024,1920]{1,0:T(8,128)(2,1)}, f32[1024,768]{1,0:T(8,128)}, f32[8,768]{1,0:T(8,128)S(1)}, f32[16,384]{1,0:T(8,128)S(1)}) custom-call(s32[2,6]{1,0:T(2,128)S(1)} %broadcast_subtract_fusion.rel_ref, f32[1024,768]{1,0:T(8,128)} %get-tuple-element.88.x_ref, f32[1024,768]{1,0:T(8,128)} %get-tuple-element.103.dmid_ref, ...), custom_call_target="tpu_custom_call" | custom-call | tf_op jit(solution)/shard_map/pallas_call | solution.py:1067
  265.0 30.4 %shard_map.162 = (bf16[1024,768]{1,0:T(8,128)(2,1)S(1)}, bf16[1024,3072]{1,0:T(8,128)(2,1)}, f32[1024,768]{1,0:T(8,128)}, bf16[1024,768]{1,0:T(8,128)(2,1)S(1)},...) custom-call(f32[1024,768]{1,0:T(8,128)} %get-tuple-element.110.dx_re, ...), custom_call_target="tpu_custom_call" | custom-call | tf_op jit(solution)/shard_map/pallas_call | solution.py:1063
  299.5 5.2 %shard_map.163.carry_ref = f32[2,8,384]{2,1,0:T(8,128)} custom-call(f32[2,8,384]{2,1,0:T(8,128)} %copy-done.31, f32[3,384]{1,0:T(4,128)} %get-tuple-element.163.rot_ref), custom_call_target="tpu_custom_call" | custom-call | tf_op jit(solution)/shard_map/pallas_call | solution.py:1066
  304.8 1.4 copy-done.21
  306.9 19.8 %shard_map.164 = (bf16[1024,1920]{1,0:T(8,128)(2,1)}, f32[1024,768]{1,0:T(8,128)}, f32[8,768]{1,0:T(8,128)S(1)}, f32[16,384]{1,0:T(8,128)S(1)}) custom-call(s32[2,6]{1,0:T(2,128)S(1)} %broadcast_subtract_fusion.rel_ref, bf16[1024,768]{1,0:T(8,128)(2,1)S(1)} %bitcast.27, f32[1024,768]{1,0:T(8,128)} %get-tuple-element.115.dmid_ref, ...), custom_call_target="tpu_custom_call" | custom-call | tf_op jit(solution)/shard_map/pallas_call | solution.py:1067
  327.4 117.3 %shard_map.165 = (bf16[2,96,1920]{2,1,0:T(8,128)(2,1)}, bf16[2,96,768]{2,1,0:T(8,128)(2,1)}, bf16[2,96,3072]{2,1,0:T(8,128)(2,1)}, bf16[2,192,768]{2,1,0:T(8,128)(2,1)}, f32[8,768]{1,0:T(8,128)}) custom-call(bf16[1024,768]{1,0:T(8,128)(2,1)} %copy-done.14, bf16[1024,768]{1,0:T(8,128)(2,1)} %copy-done.15, bf16[1024,1536]{1,0:T(8,128)(2,1)} %get-tuple-element.125.refs_2_, ...), custom_call_target="tpu_custom_call" | custom-call | tf_op jit(solution)/shard_map/pallas_call | solution.py:779
  446.8 1.9 convert_element_type.15
  448.7 2.3 convert_element_type.14
  452.1 1.7 convert_element_type.16
  (99 shorter events, 27.1 us)
Async XLA Ops:
  108.4 1.2 copy-start.2
  109.6 1.2 copy-start.10
  112.5 8.1 %copy-start = (bf16[2,512,768]{2,1,0:T(8,128)(2,1)S(1)}, bf16[2,512,768]{2,1,0:T(8,128)(2,1)}, u32[]{:S(2)}) copy-start(bf16[2,512,768]{2,1,0:T(8,128)(2,1)} %param.9) | copy-start | bytes 4718596
  112.5 8.1 %copy-start.6 = (bf16[8,96,768]{2,1,0:T(8,128)(2,1)S(1)}, bf16[8,96,768]{2,1,0:T(8,128)(2,1)}, u32[]{:S(2)}) copy-start(bf16[8,96,768]{2,1,0:T(8,128)(2,1)} %get-tuple-element.85) | copy-start | bytes 3538948
  117.9 2.7 copy-start.29
  147.4 1.2 copy-start.12
  163.8 1.2 copy-start.13
  166.7 6.9 %copy-start.8 = (bf16[8,96,768]{2,1,0:T(8,128)(2,1)S(1)}, bf16[8,96,768]{2,1,0:T(8,128)(2,1)}, u32[]{:S(2)}) copy-start(bf16[8,96,768]{2,1,0:T(8,128)(2,1)} %get-tuple-element.95) | copy-start | bytes 3538948
  172.1 1.5 copy-start.30
  173.6 26.2 %copy-start.1 = (bf16[1024,768]{1,0:T(8,128)(2,1)}, bf16[1024,768]{1,0:T(8,128)(2,1)S(1)}, u32[]{:S(2)}) copy-start(bf16[1024,768]{1,0:T(8,128)(2,1)S(1)} %slice.86.proj_ref) | copy-start | bytes 4718596
  173.6 28.6 %copy-start.9 = (bf16[8,96,768]{2,1,0:T(8,128)(2,1)S(1)}, bf16[8,96,768]{2,1,0:T(8,128)(2,1)}, u32[]{:S(2)}) copy-start(bf16[8,96,768]{2,1,0:T(8,128)(2,1)} %get-tuple-element.95) | copy-start | bytes 3538948
  201.0 1.2 copy-start.15
  202.2 39.5 %copy-start.5 = (f32[3,1024,128]{2,1,0:T(8,128)S(1)}, f32[3,1024,128]{2,1,0:T(8,128)}, u32[]{:S(2)}) copy-start(f32[3,1024,128]{2,1,0:T(8,128)} %copy-done.4) | copy-start | bytes 4718596
  233.5 1.2 copy-start.17
  234.7 1.2 copy-start.22
  241.7 1.4 copy-start.23
  243.1 1.4 copy-start.24
  245.3 19.7 %copy-start.7 = (bf16[8,96,768]{2,1,0:T(8,128)(2,1)S(1)}, bf16[8,96,768]{2,1,0:T(8,128)(2,1)}, u32[]{:S(2)}) copy-start(bf16[8,96,768]{2,1,0:T(8,128)(2,1)} %get-tuple-element.85) | copy-start | bytes 3538948
  265.0 39.7 %copy-start.3 = (f32[3,1024,128]{2,1,0:T(8,128)S(1)}, f32[3,1024,128]{2,1,0:T(8,128)}, u32[]{:S(2)}) copy-start(f32[3,1024,128]{2,1,0:T(8,128)} %copy-done.2) | copy-start | bytes 4718596
  295.4 1.2 copy-start.18
  296.6 1.2 copy-start.19
  304.7 1.4 copy-start.21
  444.7 6.3 %copy-start.36 = (bf16[2,192,768]{2,1,0:T(8,128)(2,1)S(1)}, bf16[2,192,768]{2,1,0:T(8,128)(2,1)}, u32[]{:S(2)}) copy-start(bf16[2,192,768]{2,1,0:T(8,128)(2,1)} %get-tuple-element.148) | copy-start | bytes 1769476
  446.8 5.3 %copy-start.35 = (bf16[2,96,3072]{2,1,0:T(8,128)(2,1)S(1)}, bf16[2,96,3072]{2,1,0:T(8,128)(2,1)}, u32[]{:S(2)}) copy-start(bf16[2,96,3072]{2,1,0:T(8,128)(2,1)} %get-tuple-element.147) | copy-start | bytes 3538948
  (13 other events, 11.9 us)
